TPU v7x, 32 devices: a whole 2x2x4 slice. The times are simulated.
32 devices in a mesh: replica: 2 (over x), node: 2 (over core), dev: 8 (over z, y).
Axes of the slice: x: 2, y: 2, z: 4, core: 2. Of those that a mesh axis runs over, the one named last changes fastest.
Arguments:
- tokens: bfloat16 [64, 7168], P(('replica', 'node', 'dev')), parts along dimension 0, may hold values from -6 to 6
- routes: int32 [64, 1], P(('replica', 'node', 'dev')), parts along dimension 0, may hold values from 0 to 1; in each aligned block of 2 rows (0 to 1, 2 to 3, ...) at most 2 rows name the same one
- route_weights: bfloat16 [64, 1], P(('replica', 'node', 'dev')), parts along dimension 0, may hold values from 0.049804688 to 1
- gate_weight: bfloat16 [16, 7168, 256], P(('node', 'dev')), may hold values from -0.0625 to 0.0625
- up_weight: bfloat16 [16, 7168, 256], P(('node', 'dev')), may hold values from -0.0625 to 0.0625
- down_weight: bfloat16 [16, 256, 7168], P(('node', 'dev')), may hold values from -0.125 to 0.125
Outputs:
- mixed: bfloat16 [64, 7168], P(('replica', 'node', 'dev')), parts along dimension 0
There are 2 independent parts, one for each index of `replica`. A program takes and returns all parts, laid end to end along the dimension named above; an argument that names none is the same for every part. Nothing has to cross between parts.
Inputs may be any that keep to these rules, and one draw needn't show every extreme that they name: `routes`: each row names 1 expert; among the rows of one device no expert is named by more than 2 rows, and in every draw some expert is named by exactly 2 rows of some device.
All inputs are finite; a program needn't handle non-finite values.
Results may differ from a plain program's by a relative error of at most 0.0049.
Values may be sent and summed in bfloat16 or wider, within the bound.
No kernel may reach another device: no remote copies, remote signals or barrier semaphores. Data moves between devices by JAX's collectives and lax.ppermute only.
A program may use at most 128 MiB of HBM per device.

v0:
```python
import jax
import jax.numpy as jnp
from jax import lax
from jax.sharding import PartitionSpec as P

SPLIT = 8


def place_rows(routes, weights, experts, capacity):
    tok_rows, top = routes.shape
    flat = routes.reshape(-1)
    hits = (flat[:, None] == jnp.arange(experts, dtype=jnp.int32)[None, :]).astype(jnp.int32)
    before = jnp.cumsum(hits, axis=0) - hits
    slot = jnp.sum(before * hits, axis=1)
    position = flat * capacity + slot
    table = jnp.arange(experts * capacity, dtype=jnp.int32)[:, None] == position[None, :]
    table = table.reshape(experts * capacity, tok_rows, top)
    select = jnp.any(table, axis=2).astype(jnp.float32)
    slot_weight = jnp.sum(
        jnp.where(table, weights.astype(jnp.float32)[None], jnp.float32(0.0)), axis=(1, 2)
    )
    return (select, slot_weight)


def per_device(tokens, routes, route_weights, gate_weight, up_weight, down_weight):
    tok_rows, width = tokens.shape
    top = routes.shape[1]
    nodes = lax.axis_size("node")
    devs = lax.axis_size("dev")
    per_node = devs // SPLIT
    experts = nodes * per_node
    capacity = max(2, 3 * tok_rows * top // (2 * experts))
    select, slot_weight = place_rows(routes, route_weights, experts, capacity)
    buffer = jnp.dot(
        select.astype(jnp.bfloat16), tokens, preferred_element_type=jnp.float32
    ).astype(jnp.bfloat16)
    sending = jnp.broadcast_to(
        buffer.reshape(experts, 1, capacity, width), (experts, SPLIT, capacity, width)
    )
    sending = sending.reshape(experts * SPLIT, capacity, width)
    send_weight = jnp.broadcast_to(
        slot_weight.reshape(experts, 1, capacity), (experts, SPLIT, capacity)
    )
    send_weight = send_weight.reshape(experts * SPLIT, capacity).astype(jnp.bfloat16)
    rows_in = lax.all_to_all(sending, ("node", "dev"), split_axis=0, concat_axis=0, tiled=True)
    lead = rows_in.shape[:-1]
    flat_rows = rows_in.reshape(-1, width)
    gate = jnp.dot(flat_rows, gate_weight[0], preferred_element_type=jnp.float32)
    upper = jnp.dot(flat_rows, up_weight[0], preferred_element_type=jnp.float32)
    hidden = (jax.nn.silu(gate) * upper).astype(jnp.bfloat16)
    output = jnp.dot(hidden, down_weight[0], preferred_element_type=jnp.float32)
    output = (
        output
        * lax.all_to_all(send_weight, ("node", "dev"), split_axis=0, concat_axis=0, tiled=True)
        .reshape(-1)
        .astype(jnp.float32)[:, None]
    )
    terms = output.reshape(lead + (width,))
    returned = lax.all_to_all(terms, ("node", "dev"), split_axis=0, concat_axis=0, tiled=True)
    summed = jnp.sum(returned.reshape(experts, SPLIT, capacity, width), axis=1).reshape(
        experts * capacity, width
    )
    mixed = jnp.dot(
        select.T, summed, precision=lax.Precision.HIGHEST, preferred_element_type=jnp.float32
    )
    return mixed.astype(jnp.bfloat16)


def solution(mesh):
    in_specs = (
        P(("replica", "node", "dev"), None),
        P(("replica", "node", "dev"), None),
        P(("replica", "node", "dev"), None),
        P(("node", "dev"), None, None),
        P(("node", "dev"), None, None),
        P(("node", "dev"), None, None),
    )
    out_specs = P(("replica", "node", "dev"), None)
    return jax.shard_map(
        per_device, mesh=mesh, in_specs=in_specs, out_specs=out_specs, check_vma=False
    )
```

profile of v0, /device:TPU:0, one launch (start us, length us, event | category | flops | bytes accessed | tf_op | source)
XLA Modules:
  0.0 73.8 jit_solution(11182053405740536653)
XLA Ops:
  0.0 0.8 %convert_reduce_fusion.1 = f32[2]{0:T(128)S(1)} fusion(bf16[2,1]{1,0:T(2,128)(2,1)} %param.8), kind=kLoop, calls=%fused_computation.24 | loop fusion | flops 2 | bytes 12 | tf_op jit(solution)/shard_map/convert_element_type | solution.py:20
  0.8 0.7 fusion.24
  1.5 0.8 %select_reduce_fusion = s32[2]{0:T(128)S(1)} fusion(s32[2,2]{1,0:T(2,128)S(1)} %reduce_window_sum.11, s32[2]{0:T(128)} %bitcast.30), kind=kLoop, calls=%fused_computation.27 | loop fusion | flops 18 | bytes 32 | tf_op jit(solution)/shard_map/reduce_sum | solution.py:14
  2.4 0.7 multiply_add_fusion
  3.0 0.1 fusion.21
  3.1 0.1 convert_element_type.58
  3.2 0.1 copy.13
  3.4 0.1 convert_element_type.59
  3.5 0.7 copy.14
  4.2 7.4 %all-to-all-start.1 = ((bf16[16,1,2]{2,1,0:T(2,128)(2,1)}), bf16[16,1,2]{2,1,0:T(2,128)(2,1)S(1)}, u32[]{:S(2)}, u32[]{:S(2)}) async-start(bf16[16,1,2]{2,1,0:T(2,128)(2,1)} %copy.14), calls=%async_computation.1 | async-start | bytes 16384 | tf_op jit(solution)/shard_map/all_to_all | solution.py:54
  11.6 0.2 convolution_convert_fusion
  11.8 6.1 %all-to-all-done.1 = bf16[16,1,2]{2,1,0:T(2,128)(2,1)S(1)} async-done(((bf16[16,1,2]{2,1,0:T(2,128)(2,1)}), bf16[16,1,2]{2,1,0:T(2,128)(2,1)S(1)}, u32[]{:S(2)}, u32[]{:S(2)}) %all-to-all-start.1) | async-done | bytes 96 | tf_op jit(solution)/shard_map/all_to_all | solution.py:54
  17.9 1.0 %broadcast_in_dim.30 = bf16[2,8,2,7168]{3,2,1,0:T(2,128)(2,1)} broadcast(bf16[2,2,7168]{2,1,0:T(2,128)(2,1)S(1)} %broadcast_in_dim.18), dimensions={0,2,3} | broadcast | bytes 516096 | tf_op jit(solution)/shard_map/broadcast_in_dim | solution.py:37
  18.9 3.6 %all-to-all-start = ((bf16[16,2,7168]{2,1,0:T(2,128)(2,1)}), bf16[16,2,7168]{2,1,0:T(2,128)(2,1)S(1)}, u32[]{:S(2)}, u32[]{:S(2)}) async-start(bf16[16,2,7168]{2,1,0:T(2,128)(2,1)} %bitcast.2), calls=%async_computation | async-start | bytes 917504 | tf_op jit(solution)/shard_map/all_to_all | solution.py:45
  22.5 0.1 reshape.167
  22.6 14.3 %all-to-all-done = bf16[16,2,7168]{2,1,0:T(2,128)(2,1)S(1)} async-done(((bf16[16,2,7168]{2,1,0:T(2,128)(2,1)}), bf16[16,2,7168]{2,1,0:T(2,128)(2,1)S(1)}, u32[]{:S(2)}, u32[]{:S(2)}) %all-to-all-start) | async-done | bytes 458784 | tf_op jit(solution)/shard_map/all_to_all | solution.py:45
  36.9 0.2 reshape.162
  37.0 2.8 %fusion.3 = f32[32,256]{1,0:T(8,128)S(1)} fusion(bf16[32,7168]{1,0:T(8,128)(2,1)S(1)} %reshape.162, bf16[1,7168,256]{2,1,0:T(8,128)(2,1)} %param.9), kind=kOutput, calls=%fused_computation.6 | convolution fusion | flops 117440512 | bytes 4161536 | tf_op jit(solution)/shard_map/dot_general | solution.py:48
  39.8 5.3 %convolution_multiply_fusion = f32[32,7168]{1,0:T(8,128)S(1)} fusion(bf16[1,256,7168]{2,1,0:T(8,128)(2,1)} %param.11, bf16[32,7168]{1,0:T(8,128)(2,1)S(1)} %reshape.162, bf16[1,7168,256]{2,1,0:T(8,128)(2,1)} %param.10, f32[32]{0:T(128)S(1)} %reshape.167, f32[32,256]{1,0:T(8,128)S(1)} %fusion.3), kind=kOutput, calls=%fused_computation | convolution fusion | flops 235159552 | bytes 8749184 | tf_op jit(solution)/shard_map/dot_general | solution.py:51
  45.1 0.6 reshape.163
  45.6 26.9 %all_to_all.16 = f32[16,2,7168]{2,1,0:T(2,128)S(1)} all-to-all(f32[16,2,7168]{2,1,0:T(2,128)S(1)} %reshape.163), channel_id=1, replica_groups=mesh['replica'=2,'node'=2,'dev'=8] {'node','dev'}, dimensions={0} | all-to-all | bytes 1835008 | tf_op jit(solution)/shard_map/all_to_all | solution.py:59
  72.5 0.2 bitcast_reduce_fusion
  72.7 0.1 reshape.165
  72.8 0.9 %convolution_convert_fusion.1 = bf16[2,7168]{1,0:T(2,128)(2,1)} fusion(f32[4,7168]{1,0:T(4,128)S(1)} %reshape.165, s32[2]{0:T(128)S(1)} %multiply_add_fusion), kind=kOutput, calls=%fused_computation.2 | convolution fusion | flops 702472 | bytes 143368 | tf_op jit(solution)/shard_map/dot_general | solution.py:63
  (6 shorter events, 0.2 us)
Async XLA Ops:
  0.0 11.6 %copy-start = (bf16[2,7168]{1,0:T(2,128)(2,1)S(1)}, bf16[2,7168]{1,0:T(2,128)(2,1)}, u32[]{:S(2)}) copy-start(bf16[2,7168]{1,0:T(2,128)(2,1)} %param.6) | copy-start | bytes 86020
  4.2 13.7 %all-to-all-start.1 = ((bf16[16,1,2]{2,1,0:T(2,128)(2,1)}), bf16[16,1,2]{2,1,0:T(2,128)(2,1)S(1)}, u32[]{:S(2)}, u32[]{:S(2)}) async-start(bf16[16,1,2]{2,1,0:T(2,128)(2,1)} %copy.14), calls=%async_computation.1 | async-start | bytes 16384 | tf_op jit(solution)/shard_map/all_to_all | solution.py:54
  18.9 17.9 %all-to-all-start = ((bf16[16,2,7168]{2,1,0:T(2,128)(2,1)}), bf16[16,2,7168]{2,1,0:T(2,128)(2,1)S(1)}, u32[]{:S(2)}, u32[]{:S(2)}) async-start(bf16[16,2,7168]{2,1,0:T(2,128)(2,1)} %bitcast.2), calls=%async_computation | async-start | bytes 917504 | tf_op jit(solution)/shard_map/all_to_all | solution.py:45
where the time goes:
time: 74.2 us; the launch traced here: 73.8 us
  blocking collectives  26.9 us (36%)
  waiting for transfers between devices  20.4 us (27%)
  starting transfers between devices  10.9 us (15%)
  matrix products  9.11 us (12%)
  other arithmetic  3.37 us (5%)
  local copies, waits for them, and re-layouts  3.01 us (4%)
    all_to_all x1, blocking collectives, per_device(): lax.all_to_all(terms, ('node', 'dev'), split_axis=0, concat_axis=0, tiled...  26.9 us
    all_to_all x1, waiting for transfers between devices, per_device(): lax.all_to_all(sending, ('node', 'dev'), split_axis=0, concat_axis=0, til...  14.3 us
    all_to_all x1, starting transfers between devices, per_device(): lax.all_to_all(send_weight, ('node', 'dev'), split_axis=0, concat_axis=0,...  7.39 us
    all_to_all x1, waiting for transfers between devices, per_device(): lax.all_to_all(send_weight, ('node', 'dev'), split_axis=0, concat_axis=0,...  6.1 us
    dot_general x1, matrix products, per_device(): output = jnp.dot(hidden, down_weight[0], preferred_element_type=jnp.float32)  5.25 us
    all_to_all x1, starting transfers between devices, per_device(): lax.all_to_all(sending, ('node', 'dev'), split_axis=0, concat_axis=0, til...  3.56 us
    dot_general x1, matrix products, per_device(): jnp.dot(flat_rows, gate_weight[0], preferred_element_type=jnp.float32)  2.77 us
  transfers between devices with their start and end apart: 2, of which 2 were waited for; matrix products, arithmetic and copies ran while one was open for 0% of the time, Pallas kernels for 0%

commit v1 on v0

v1 whole, which is shorter than its diff:
```python
import functools

import jax
import jax.numpy as jnp
from jax import lax
from jax.experimental import pallas as pl
from jax.experimental.pallas import tpu as pltpu
from jax.sharding import PartitionSpec as P

SPLIT = 8
LANES = 128
VMEM_LIMIT = 48 * 1024 * 1024


def pack_kernel(tokens_ref, routes_ref, weights_ref, packed_ref):
    rows, width = tokens_ref.shape
    copies = packed_ref.shape[0]
    extra = packed_ref.shape[2] - width
    columns = lax.broadcasted_iota(jnp.int32, (rows, extra), 1)
    combine = jnp.zeros((rows, extra), jnp.float32)
    for k in range(routes_ref.shape[1]):
        chosen = columns == routes_ref[:, k : k + 1]
        combine += jnp.where(chosen, weights_ref[:, k : k + 1].astype(jnp.float32), 0.0)
    combine = combine.astype(jnp.bfloat16)
    for c in range(copies):
        packed_ref[c, :, :width] = tokens_ref[...]
        packed_ref[c, :, width:] = combine


def expert_kernel(
    expert_ref, own_ref, other_ref, gate_hbm, up_hbm, down_hbm, own_out, other_out,
    gate_buf, up_buf, down_buf, gate_sem, up_sem, down_sem,
):
    rows = own_ref.shape[0]
    width, hidden_units = gate_buf.shape
    steps = gate_sem.shape[0]
    tall = width // steps

    def gate_copy(i):
        part = pl.ds(i * tall, tall)
        return pltpu.make_async_copy(gate_hbm.at[0, part], gate_buf.at[part], gate_sem.at[i])

    def up_copy(i):
        part = pl.ds(i * tall, tall)
        return pltpu.make_async_copy(up_hbm.at[0, part], up_buf.at[part], up_sem.at[i])

    def down_copy(i):
        part = pl.ds(i * tall, tall)
        return pltpu.make_async_copy(
            down_hbm.at[0, :, part], down_buf.at[:, part], down_sem.at[i]
        )

    for i in range(steps):
        gate_copy(i).start()
        up_copy(i).start()
    for i in range(steps):
        down_copy(i).start()

    combine = jnp.concatenate([own_ref[:, width:], other_ref[:, width:]], axis=0)
    columns = lax.broadcasted_iota(jnp.int32, combine.shape, 1)
    scale = jnp.sum(
        jnp.where(columns == expert_ref[0], combine.astype(jnp.float32), 0.0),
        axis=1, keepdims=True,
    )
    gate = jnp.zeros((2 * rows, hidden_units), jnp.float32)
    upper = jnp.zeros((2 * rows, hidden_units), jnp.float32)
    for i in range(steps):
        part = slice(i * tall, (i + 1) * tall)
        block = jnp.concatenate([own_ref[:, part], other_ref[:, part]], axis=0)
        gate_copy(i).wait()
        gate += jnp.dot(block, gate_buf[part, :], preferred_element_type=jnp.float32)
        up_copy(i).wait()
        upper += jnp.dot(block, up_buf[part, :], preferred_element_type=jnp.float32)
    hidden = (gate / (1.0 + jnp.exp(-gate)) * upper).astype(jnp.bfloat16)
    for i in range(steps):
        part = slice(i * tall, (i + 1) * tall)
        down_copy(i).wait()
        output = scale * jnp.dot(
            hidden, down_buf[:, part], preferred_element_type=jnp.float32
        )
        own_out[:, part] = output[:rows].astype(own_out.dtype)
        other_out[:, part] = output[rows:].astype(other_out.dtype)


def per_device(tokens, routes, route_weights, gate_weight, up_weight, down_weight):
    tok_rows, width = tokens.shape
    hidden_units = gate_weight.shape[2]
    nodes = lax.axis_size("node")
    devs = lax.axis_size("dev")
    per_node = devs // SPLIT
    experts = nodes * per_node
    wide = width + -(-experts // LANES) * LANES
    rows = devs * tok_rows
    vmem = pl.BlockSpec(memory_space=pltpu.VMEM)
    anywhere = pl.BlockSpec(memory_space=pl.ANY)
    swap = [(i, i ^ 1) for i in range(nodes)]

    packed = pl.pallas_call(
        pack_kernel,
        out_shape=jax.ShapeDtypeStruct((devs, tok_rows, wide), jnp.bfloat16),
        in_specs=[vmem] * 3,
        out_specs=vmem,
        name="pack",
    )(tokens, routes, route_weights)
    own = lax.all_to_all(packed, "dev", split_axis=0, concat_axis=0, tiled=True)
    own = own.reshape(rows, wide)
    other = lax.ppermute(own, "node", swap)

    expert = lax.axis_index("node") * per_node + lax.axis_index("dev") // SPLIT
    steps = 7
    own_out, other_out = pl.pallas_call(
        expert_kernel,
        out_shape=(
            jax.ShapeDtypeStruct((rows, width), jnp.float32),
            jax.ShapeDtypeStruct((rows, width), jnp.bfloat16),
        ),
        in_specs=[pl.BlockSpec(memory_space=pltpu.SMEM), vmem, vmem] + [anywhere] * 3,
        out_specs=(vmem, vmem),
        scratch_shapes=[
            pltpu.VMEM((width, hidden_units), jnp.bfloat16),
            pltpu.VMEM((width, hidden_units), jnp.bfloat16),
            pltpu.VMEM((hidden_units, width), jnp.bfloat16),
            pltpu.SemaphoreType.DMA((steps,)),
            pltpu.SemaphoreType.DMA((steps,)),
            pltpu.SemaphoreType.DMA((steps,)),
        ],
        compiler_params=pltpu.CompilerParams(vmem_limit_bytes=VMEM_LIMIT),
        name="expert",
    )(expert.reshape(1).astype(jnp.int32), own, other, gate_weight, up_weight, down_weight)
    arrived = lax.ppermute(other_out, "node", swap)
    partial = (own_out + arrived.astype(jnp.float32)).astype(jnp.bfloat16)
    returned = lax.all_to_all(
        partial.reshape(devs, tok_rows, width), "dev", split_axis=0, concat_axis=0, tiled=True
    )
    return jnp.sum(returned.astype(jnp.float32), axis=0).astype(jnp.bfloat16)


def solution(mesh):
    rows = P(("replica", "node", "dev"), None)
    shards = P(("node", "dev"), None, None)
    return jax.shard_map(
        per_device,
        mesh=mesh,
        in_specs=(rows, rows, rows, shards, shards, shards),
        out_specs=rows,
        check_vma=False,
    )
```

time: 74.2 us -> 42 us (0.57)
  waiting for transfers between devices: 20.4 us -> 2.82 us
  starting transfers between devices: 10.9 us -> 0.27 us
  matrix products: 9.11 us -> 0 us
  Pallas kernels: 0 us -> 6.45 us
  other arithmetic: 3.37 us -> 0.86 us
  blocking collectives: 26.9 us -> 27.7 us
    all_to_all x2 -> x0, waiting for transfers between devices: 20.4 us -> none  [the longest x1 14.3 us: per_device(): lax.all_to_all(sending, ('node', 'dev'), split_axis=0, concat_axis=0, til...]
    all_to_all x2 -> x0, starting transfers between devices: 10.9 us -> none  [the longest x1 7.39 us: per_device(): lax.all_to_all(send_weight, ('node', 'dev'), split_axis=0, concat_axis=0,...]
    dot_general x4 -> x0, matrix products: 9.11 us -> none  [the longest x1 5.25 us: per_device(): output = jnp.dot(hidden, down_weight[0], preferred_element_type=jnp.float32)]
    pallas_call x0 -> x2, Pallas kernels: none -> 6.45 us  [the longest x1 4.92 us: per_device(): pl.pallas_call(expert_kernel, out_shape=(jax.ShapeDtypeStruct((rows, widt...]
    unnamed x2 -> x3, local copies, waits for them, and re-layouts: 0.01 us -> 3.33 us
    ppermute x0 -> x2, waiting for transfers between devices: none -> 2.82 us  [the longest x1 1.47 us: per_device(): other = lax.ppermute(own, 'node', swap)]
    convert_element_type x3 -> x1, other arithmetic: 1.53 us -> 0.04 us  [per_device(): partial = (own_out + arrived.astype(jnp.float32)).astype(jnp.bfloat16)]
    broadcast_in_dim x3 -> x0, local copies, waits for them, and re-layouts: 1.11 us -> none  [the longest x2 1.04 us: per_device(): jnp.broadcast_to(buffer.reshape(experts, 1, capacity, width), (experts, S...]
where the time goes in v1:
time: 42 us; the launch traced here: 41.7 us
  blocking collectives  27.7 us (66%)
  Pallas kernels  6.45 us (15%)
  local copies, waits for them, and re-layouts  3.51 us (8%)
  waiting for transfers between devices  2.82 us (7%)
  other arithmetic  0.86 us (2%)
    all_to_all x1, blocking collectives, per_device(): own = lax.all_to_all(packed, 'dev', split_axis=0, concat_axis=0, tiled=True)  15.8 us
    all_to_all x1, blocking collectives, per_device(): lax.all_to_all(partial.reshape(devs, tok_rows, width), 'dev', split_axis=...  11.9 us
    pallas_call x1, Pallas kernels, per_device(): pl.pallas_call(expert_kernel, out_shape=(jax.ShapeDtypeStruct((rows, widt...  4.92 us
    unnamed x3, local copies, waits for them, and re-layouts  3.33 us
    pallas_call x1, Pallas kernels, per_device(): pl.pallas_call(pack_kernel, out_shape=jax.ShapeDtypeStruct((devs, tok_row...  1.53 us
    ppermute x1, waiting for transfers between devices, per_device(): other = lax.ppermute(own, 'node', swap)  1.47 us
    ppermute x1, waiting for transfers between devices, per_device(): arrived = lax.ppermute(other_out, 'node', swap)  1.35 us
  transfers between devices with their start and end apart: 2, of which 2 were waited for; matrix products, arithmetic and copies ran while one was open for 0% of the time, Pallas kernels for 0%

profile of v1, /device:TPU:0, one launch (start us, length us, event | category | flops | bytes accessed | tf_op | source)
XLA Modules:
  0.0 41.7 jit_solution(12868715555802823794)
XLA Ops:
  0.0 1.3 %copy.7.routes_ref = s32[2,1]{1,0:T(2,128)} copy(s32[2,1]{0,1:T(1,128)} %param.7) | data formatting | bytes 16 | tf_op args[1]
  1.3 1.5 %pack.1 = bf16[8,2,7296]{2,1,0:T(2,128)(2,1)} custom-call(bf16[2,7168]{1,0:T(2,128)(2,1)} %tokens_ref.1, s32[2,1]{1,0:T(2,128)} %copy.7.routes_ref, bf16[2,1]{1,0:T(2,128)(2,1)} %weights_ref.1), custom_call_target="tpu_custom_call" | custom-call | tf_op jit(solution)/shard_map/pack/pallas_call | solution.py:98
  2.8 15.8 %all_to_all.10 = bf16[8,2,7296]{2,1,0:T(2,128)(2,1)S(1)} all-to-all(bf16[8,2,7296]{2,1,0:T(2,128)(2,1)} %pack.1), channel_id=1, replica_groups=mesh['replica'=2,'node'=2,'dev'=8] {'dev'}, dimensions={0} | all-to-all | bytes 466944 | tf_op jit(solution)/shard_map/all_to_all | solution.py:105
  18.6 0.1 reshape.10.own_ref
  18.7 0.1 collective-permute-start
  18.8 1.5 %collective-permute-done.other_ref = bf16[16,7296]{1,0:T(8,128)(2,1)S(1)} collective-permute-done((bf16[16,7296]{1,0:T(8,128)(2,1)S(1)}, bf16[16,7296]{1,0:T(8,128)(2,1)S(1)}, u32[]{:S(2)}, u32[]{:S(2)}) %collective-permute-start) | collective-permute-done | bytes 233504 | tf_op jit(solution)/shard_map/ppermute | solution.py:107
  20.3 0.0 copy-start
  20.3 2.0 %copy-done = bf16[1,7168,256]{2,1,0:T(8,128)(2,1)S(1)} copy-done((bf16[1,7168,256]{2,1,0:T(8,128)(2,1)S(1)}, bf16[1,7168,256]{2,1,0:T(8,128)(2,1)}, u32[]{:S(2)}) %copy-start) | copy-done | bytes 3670040
  22.3 4.9 %expert.1 = (f32[16,7168]{1,0:T(8,128)S(1)}, bf16[16,7168]{1,0:T(8,128)(2,1)S(1)}) custom-call(s32[1]{0:T(128)} %bitcast.expert_ref, bf16[16,7296]{1,0:T(8,128)(2,1)S(1)} %reshape.10.own_ref, bf16[16,7296]{1,0:T(8,128)(2,1)S(1)} %collective-permute-done.other_ref, bf16[1,7168,256]{2,1,0:T(8,128)(2,1)S(1)} %copy-done, bf16[1,7168,256]{2,1,0:T(8,128)(2,1)} %up_hbm.1, ...), custom_call_target="tpu_custom_call" | custom-call | tf_op jit(solution)/shard_map/expert/pallas_call | solution.py:111
  27.2 0.2 collective-permute-start.1
  27.4 1.4 %collective-permute-done.1 = bf16[16,7168]{1,0:T(8,128)(2,1)S(1)} collective-permute-done((bf16[16,7168]{1,0:T(8,128)(2,1)S(1)}, bf16[16,7168]{1,0:T(8,128)(2,1)S(1)}, u32[]{:S(2)}, u32[]{:S(2)}) %collective-permute-start.1) | collective-permute-done | bytes 229408 | tf_op jit(solution)/shard_map/ppermute | solution.py:130
  28.8 0.1 reshape.11
  28.9 11.9 %all_to_all.11 = bf16[8,2,7168]{2,1,0:T(2,128)(2,1)S(1)} all-to-all(bf16[8,2,7168]{2,1,0:T(2,128)(2,1)S(1)} %reshape.11), channel_id=1, replica_groups=mesh['replica'=2,'node'=2,'dev'=8] {'dev'}, dimensions={0} | all-to-all | bytes 458752 | tf_op jit(solution)/shard_map/all_to_all | solution.py:132
  40.9 0.8 %reduce_sum.12 = bf16[2,7168]{1,0:T(2,128)(2,1)} reduce(bf16[8,2,7168]{2,1,0:T(2,128)(2,1)S(1)} %all_to_all.11, bf16[]{:T(256)} %constant.27.clone.1), dimensions={0}, to_apply=%region_0.1 | reduce | flops 100352 | bytes 258050 | tf_op jit(solution)/shard_map/reduce_sum | solution.py:135
  (1 shorter events, 0.0 us)
Async XLA Ops:
  18.7 1.6 %collective-permute-start = (bf16[16,7296]{1,0:T(8,128)(2,1)S(1)}, bf16[16,7296]{1,0:T(8,128)(2,1)S(1)}, u32[]{:S(2)}, u32[]{:S(2)}) collective-permute-start(bf16[16,7296]{1,0:T(8,128)(2,1)S(1)} %reshape.10.own_ref), channel_id=1, source_target_pairs={{0,8},{8,0},{1,9},{9,1},{2,10},{10,2},{3,11},{11,3},{4,12},{12,4},... | collective-permute-start | bytes 700424 | tf_op jit(solution)/shard_map/ppermute | solution.py:107
  20.3 2.0 %copy-start = (bf16[1,7168,256]{2,1,0:T(8,128)(2,1)S(1)}, bf16[1,7168,256]{2,1,0:T(8,128)(2,1)}, u32[]{:S(2)}) copy-start(bf16[1,7168,256]{2,1,0:T(8,128)(2,1)} %gate_hbm.1) | copy-start | bytes 11010052
  27.2 1.6 %collective-permute-start.1 = (bf16[16,7168]{1,0:T(8,128)(2,1)S(1)}, bf16[16,7168]{1,0:T(8,128)(2,1)S(1)}, u32[]{:S(2)}, u32[]{:S(2)}) collective-permute-start(bf16[16,7168]{1,0:T(8,128)(2,1)S(1)} %get-tuple-element.8), channel_id=1, source_target_pairs={{0,8},{8,0},{1,9},{9,1},{2,10},{10,2},{3,11},{11,3},{4,12},{12,4},... | collective-permute-start | bytes 688136 | tf_op jit(solution)/shard_map/ppermute | solution.py:130

commit v2 on v1

v2 whole, which is shorter than its diff:
```python
import jax
import jax.numpy as jnp
from jax import lax
from jax.experimental import pallas as pl
from jax.experimental.pallas import tpu as pltpu
from jax.sharding import PartitionSpec as P

SPLIT = 8
LANES = 128
LOAD_LIMIT = 48 * 1024 * 1024
HEAD = 5632
DOWN_STEP = 1792
COLUMNS = 512


def pack_kernel(tokens_ref, routes_ref, weights_ref, packed_ref):
    rows, width = tokens_ref.shape
    copies = packed_ref.shape[0]
    extra = packed_ref.shape[2] - width
    columns = lax.broadcasted_iota(jnp.int32, (rows, extra), 1)
    combine = jnp.zeros((rows, extra), jnp.float32)
    for k in range(routes_ref.shape[0]):
        route = jnp.concatenate([routes_ref[k : k + 1, r : r + 1] for r in range(rows)], axis=0)
        weight = weights_ref[:, k : k + 1].astype(jnp.float32)
        combine += jnp.where(columns == route, weight, 0.0)
    combine = combine.astype(jnp.bfloat16)
    for c in range(copies):
        packed_ref[c, :, :width] = tokens_ref[...]
        packed_ref[c, :, width:] = combine


def load_kernel(weight_hbm, part_ref, sem):
    head = pl.ds(0, part_ref.shape[0])
    copy = pltpu.make_async_copy(weight_hbm.at[0, head], part_ref, sem)
    copy.start()
    copy.wait()


def expert_kernel(
    own_ref, other_ref, gate_head, up_head, gate_hbm, up_hbm, down_hbm, own_out, other_out,
    gate_tail, up_tail, down_buf, gate_sem, up_sem, down_sem,
):
    rows = own_ref.shape[0]
    head, hidden_units = gate_head.shape
    width = own_out.shape[1]
    rest = pl.ds(head, width - head)
    gate_copy = pltpu.make_async_copy(gate_hbm.at[0, rest], gate_tail, gate_sem)
    up_copy = pltpu.make_async_copy(up_hbm.at[0, rest], up_tail, up_sem)

    def down_copy(i):
        part = pl.ds(i * DOWN_STEP, DOWN_STEP)
        return pltpu.make_async_copy(
            down_hbm.at[0, :, part], down_buf.at[:, part], down_sem.at[i]
        )

    gate_copy.start()
    up_copy.start()
    for i in range(width // DOWN_STEP):
        down_copy(i).start()

    expert = lax.axis_index("node") * (lax.axis_size("dev") // SPLIT) + lax.axis_index("dev") // SPLIT
    combine = jnp.concatenate([own_ref[:, width:], other_ref[:, width:]], axis=0)
    columns = lax.broadcasted_iota(jnp.int32, combine.shape, 1)
    scale = jnp.sum(
        jnp.where(columns == expert, combine.astype(jnp.float32), 0.0), axis=1, keepdims=True
    )
    gate = jnp.zeros((2 * rows, hidden_units), jnp.float32)
    upper = jnp.zeros((2 * rows, hidden_units), jnp.float32)
    for start in range(0, head, COLUMNS):
        part = slice(start, start + COLUMNS)
        block = jnp.concatenate([own_ref[:, part], other_ref[:, part]], axis=0)
        gate += jnp.dot(block, gate_head[part, :], preferred_element_type=jnp.float32)
        upper += jnp.dot(block, up_head[part, :], preferred_element_type=jnp.float32)
    block = jnp.concatenate([own_ref[:, head:width], other_ref[:, head:width]], axis=0)
    gate_copy.wait()
    gate += jnp.dot(block, gate_tail[...], preferred_element_type=jnp.float32)
    up_copy.wait()
    upper += jnp.dot(block, up_tail[...], preferred_element_type=jnp.float32)
    hidden = (gate / (1.0 + jnp.exp(-gate)) * upper).astype(jnp.bfloat16)
    for i in range(width // DOWN_STEP):
        part = slice(i * DOWN_STEP, (i + 1) * DOWN_STEP)
        down_copy(i).wait()
        output = scale * jnp.dot(
            hidden, down_buf[:, part], preferred_element_type=jnp.float32
        )
        own_out[:, part] = output[:rows].astype(own_out.dtype)
        other_out[:, part] = output[rows:].astype(other_out.dtype)


def load_head(weight):
    part = (HEAD, weight.shape[2])
    return pl.pallas_call(
        load_kernel,
        out_shape=pltpu.VMEM(part, weight.dtype),
        in_specs=[pl.BlockSpec(memory_space=pltpu.HBM)],
        out_specs=pl.BlockSpec(memory_space=pltpu.VMEM),
        scratch_shapes=[pltpu.SemaphoreType.DMA],
        compiler_params=pltpu.CompilerParams(vmem_limit_bytes=LOAD_LIMIT),
        cost_estimate=pl.CostEstimate(
            flops=0, transcendentals=0, bytes_accessed=2 * part[0] * part[1]
        ),
        name="load",
    )(weight)


def per_device(tokens, routes, route_weights, gate_weight, up_weight, down_weight):
    tok_rows, width = tokens.shape
    hidden_units = gate_weight.shape[2]
    nodes = lax.axis_size("node")
    devs = lax.axis_size("dev")
    per_node = devs // SPLIT
    experts = nodes * per_node
    wide = width + -(-experts // LANES) * LANES
    rows = devs * tok_rows
    vmem = pl.BlockSpec(memory_space=pltpu.VMEM)
    swap = [(i, i ^ 1) for i in range(nodes)]

    packed = pl.pallas_call(
        pack_kernel,
        out_shape=jax.ShapeDtypeStruct((devs, tok_rows, wide), jnp.bfloat16),
        in_specs=[vmem] * 3,
        out_specs=vmem,
        name="pack",
    )(tokens, routes.T, route_weights)
    own = lax.all_to_all(packed, "dev", split_axis=0, concat_axis=0, tiled=True)
    gate_head = load_head(gate_weight)
    own, gate_head = lax.optimization_barrier((own, gate_head))
    own = own.reshape(rows, wide)
    own, up_source = lax.optimization_barrier((own, up_weight))
    other = lax.ppermute(own, "node", swap)
    up_head = load_head(up_source)
    other, up_head = lax.optimization_barrier((other, up_head))
    tail = (width - HEAD, hidden_units)
    resident = 2 * (2 * rows * wide + 2 * HEAD * hidden_units) + 6 * rows * width
    own_out, other_out = pl.pallas_call(
        expert_kernel,
        out_shape=(
            jax.ShapeDtypeStruct((rows, width), jnp.float32),
            jax.ShapeDtypeStruct((rows, width), jnp.bfloat16),
        ),
        in_specs=[vmem] * 4 + [pl.BlockSpec(memory_space=pltpu.HBM)] * 3,
        out_specs=(vmem, vmem),
        scratch_shapes=[
            pltpu.VMEM(tail, jnp.bfloat16),
            pltpu.VMEM(tail, jnp.bfloat16),
            pltpu.VMEM((hidden_units, width), jnp.bfloat16),
            pltpu.SemaphoreType.DMA,
            pltpu.SemaphoreType.DMA,
            pltpu.SemaphoreType.DMA((width // DOWN_STEP,)),
        ],
        compiler_params=pltpu.CompilerParams(
            vmem_limit_bytes=52 * 1024 * 1024 - resident
        ),
        name="expert",
    )(own, other, gate_head, up_head, gate_weight, up_weight, down_weight)
    arrived = lax.ppermute(other_out, "node", swap)
    partial = (own_out + arrived.astype(jnp.float32)).astype(jnp.bfloat16)
    returned = lax.all_to_all(
        partial.reshape(devs, tok_rows, width), "dev", split_axis=0, concat_axis=0, tiled=True
    )
    return jnp.sum(returned.astype(jnp.float32), axis=0).astype(jnp.bfloat16)


def solution(mesh):
    rows = P(("replica", "node", "dev"), None)
    shards = P(("node", "dev"), None, None)
    return jax.shard_map(
        per_device,
        mesh=mesh,
        in_specs=(rows, rows, rows, shards, shards, shards),
        out_specs=rows,
        check_vma=False,
    )
```

time: 42 us -> 38.9 us (0.926)
  blocking collectives: 27.7 us -> 12.2 us
  starting transfers between devices: 0.27 us -> 7.91 us
  waiting for transfers between devices: 2.82 us -> 7.78 us
  local copies, waits for them, and re-layouts: 3.51 us -> 0.18 us
  Pallas kernels: 6.45 us -> 9.52 us
    all_to_all x1 -> x0, blocking collectives: 15.8 us -> none  [per_device(): own = lax.all_to_all(packed, 'dev', split_axis=0, concat_axis=0, tiled=True)]
    all_to_all x0 -> x1, starting transfers between devices: none -> 7.28 us  [per_device(): own = lax.all_to_all(packed, 'dev', split_axis=0, concat_axis=0, tiled=True)]
    all_to_all x0 -> x1, waiting for transfers between devices: none -> 6.67 us  [per_device(): own = lax.all_to_all(packed, 'dev', split_axis=0, concat_axis=0, tiled=True)]
    pallas_call x0 -> x2, Pallas kernels: none -> 3.65 us  [load_head(): pl.pallas_call(load_kernel, out_shape=pltpu.VMEM(part, weight.dtype), in_...]
    unnamed x3 -> x0, local copies, waits for them, and re-layouts: 3.33 us -> none
    ppermute x1, waiting for transfers between devices: 1.47 us -> 0.01 us  [per_device(): other = lax.ppermute(own, 'node', swap)]
    pallas_call x1, Pallas kernels: 4.92 us -> 4.28 us  [per_device(): pl.pallas_call(expert_kernel, out_shape=(jax.ShapeDtypeStruct((rows, widt...]
  transfers between devices with their start and end apart: 2 -> 3, of which waited for: 2 -> 2; matrix products, arithmetic and copies ran while one was open for 0% -> 0% of each run, Pallas kernels for 0% -> 9%
where the time goes in v2:
time: 38.9 us; the launch traced here: 38.5 us
  blocking collectives  12.2 us (31%)
  Pallas kernels  9.52 us (24%)
  starting transfers between devices  7.91 us (20%)
  waiting for transfers between devices  7.78 us (20%)
  other arithmetic  0.86 us (2%)
    all_to_all x1, blocking collectives, per_device(): lax.all_to_all(partial.reshape(devs, tok_rows, width), 'dev', split_axis=...  12.2 us
    all_to_all x1, starting transfers between devices, per_device(): own = lax.all_to_all(packed, 'dev', split_axis=0, concat_axis=0, tiled=True)  7.28 us
    all_to_all x1, waiting for transfers between devices, per_device(): own = lax.all_to_all(packed, 'dev', split_axis=0, concat_axis=0, tiled=True)  6.67 us
    pallas_call x1, Pallas kernels, per_device(): pl.pallas_call(expert_kernel, out_shape=(jax.ShapeDtypeStruct((rows, widt...  4.28 us
    pallas_call x2, Pallas kernels, load_head(): pl.pallas_call(load_kernel, out_shape=pltpu.VMEM(part, weight.dtype), in_...  3.65 us
    pallas_call x1, Pallas kernels, per_device(): pl.pallas_call(pack_kernel, out_shape=jax.ShapeDtypeStruct((devs, tok_row...  1.59 us
    ppermute x1, waiting for transfers between devices, per_device(): arrived = lax.ppermute(other_out, 'node', swap)  1.12 us
    reduce_sum x1, other arithmetic, per_device(): return jnp.sum(returned.astype(jnp.float32), axis=0).astype(jnp.bfloat16)  0.82 us
  transfers between devices with their start and end apart: 3, of which 2 were waited for; matrix products, arithmetic and copies ran while one was open for 0% of the time, Pallas kernels for 9%

profile of v2, /device:TPU:0, one launch (start us, length us, event | category | flops | bytes accessed | tf_op | source)
XLA Modules:
  0.0 38.5 jit_solution(16392644978480089415)
XLA Ops:
  0.0 1.6 %pack.1 = bf16[8,2,7296]{2,1,0:T(2,128)(2,1)} custom-call(bf16[2,7168]{1,0:T(2,128)(2,1)} %tokens_ref.1, s32[1,2]{1,0:T(1,128)} %bitcast.1, bf16[2,1]{1,0:T(2,128)(2,1)} %weights_ref.1), custom_call_target="tpu_custom_call" | custom-call | tf_op jit(solution)/shard_map/pack/pallas_call | solution.py:118
  1.6 7.3 %all-to-all-start = ((bf16[8,2,7296]{2,1,0:T(2,128)(2,1)}), bf16[8,2,7296]{2,1,0:T(2,128)(2,1)S(1)}, u32[]{:S(2)}, u32[]{:S(2)}) async-start(bf16[8,2,7296]{2,1,0:T(2,128)(2,1)} %pack.1), calls=%async_computation | async-start | bytes 466944 | tf_op jit(solution)/shard_map/all_to_all | solution.py:125
  8.9 1.8 %load.2.gate_head = bf16[5632,256]{1,0:T(8,128)(2,1)S(1)} custom-call(bf16[1,7168,256]{2,1,0:T(8,128)(2,1)} %gate_hbm.1), custom_call_target="tpu_custom_call" | custom-call | bytes 2883584 | tf_op jit(solution)/shard_map/load/pallas_call | solution.py:92
  10.7 6.7 %all-to-all-done = bf16[8,2,7296]{2,1,0:T(2,128)(2,1)S(1)} async-done(((bf16[8,2,7296]{2,1,0:T(2,128)(2,1)}), bf16[8,2,7296]{2,1,0:T(2,128)(2,1)S(1)}, u32[]{:S(2)}, u32[]{:S(2)}) %all-to-all-start) | async-done | bytes 233504 | tf_op jit(solution)/shard_map/all_to_all | solution.py:125
  17.4 0.1 reshape.6.own_ref
  17.5 0.1 collective-permute-start
  17.5 1.8 %load.3.up_head = bf16[5632,256]{1,0:T(8,128)(2,1)S(1)} custom-call(bf16[1,7168,256]{2,1,0:T(8,128)(2,1)} %up_hbm.1), custom_call_target="tpu_custom_call" | custom-call | bytes 2883584 | tf_op jit(solution)/shard_map/load/pallas_call | solution.py:92
  19.4 0.0 collective-permute-done.other_ref
  19.4 4.3 %expert.1 = (f32[16,7168]{1,0:T(8,128)S(1)}, bf16[16,7168]{1,0:T(8,128)(2,1)S(1)}) custom-call(bf16[16,7296]{1,0:T(8,128)(2,1)S(1)} %reshape.6.own_ref, bf16[16,7296]{1,0:T(8,128)(2,1)S(1)} %collective-permute-done.other_ref, bf16[5632,256]{1,0:T(8,128)(2,1)S(1)} %load.2.gate_head, bf16[5632,256]{1,0:T(8,128)(2,1)S(1)} %load.3.up_head, ...), custom_call_target="tpu_custom_call" | custom-call | tf_op jit(solution)/shard_map/expert/pallas_call | solution.py:135
  23.7 0.6 %collective-permute-start.1 = (bf16[16,7168]{1,0:T(8,128)(2,1)S(1)}, bf16[16,7168]{1,0:T(8,128)(2,1)S(1)}, u32[]{:S(2)}, u32[]{:S(2)}) collective-permute-start(bf16[16,7168]{1,0:T(8,128)(2,1)S(1)} %get-tuple-element.20), channel_id=1, source_target_pairs={{0,8},{8,0},{1,9},{9,1},{2,10},{10,2},{3,11},{11,3},{4,12},{12,4},... | collective-permute-start | bytes 688136 | tf_op jit(solution)/shard_map/ppermute | solution.py:156
  24.2 1.1 %collective-permute-done.1 = bf16[16,7168]{1,0:T(8,128)(2,1)S(1)} collective-permute-done((bf16[16,7168]{1,0:T(8,128)(2,1)S(1)}, bf16[16,7168]{1,0:T(8,128)(2,1)S(1)}, u32[]{:S(2)}, u32[]{:S(2)}) %collective-permute-start.1) | collective-permute-done | bytes 229408 | tf_op jit(solution)/shard_map/ppermute | solution.py:156
  25.4 0.1 reshape.7
  25.5 12.2 %all_to_all.10 = bf16[8,2,7168]{2,1,0:T(2,128)(2,1)S(1)} all-to-all(bf16[8,2,7168]{2,1,0:T(2,128)(2,1)S(1)} %reshape.7), channel_id=1, replica_groups=mesh['replica'=2,'node'=2,'dev'=8] {'dev'}, dimensions={0} | all-to-all | bytes 458752 | tf_op jit(solution)/shard_map/all_to_all | solution.py:158
  37.7 0.8 %reduce_sum.12 = bf16[2,7168]{1,0:T(2,128)(2,1)} reduce(bf16[8,2,7168]{2,1,0:T(2,128)(2,1)S(1)} %all_to_all.10, bf16[]{:T(256)} %constant.2.clone.1), dimensions={0}, to_apply=%region_0.0 | reduce | flops 100352 | bytes 258050 | tf_op jit(solution)/shard_map/reduce_sum | solution.py:161
  (1 shorter events, 0.0 us)
Async XLA Ops:
  1.6 15.8 %all-to-all-start = ((bf16[8,2,7296]{2,1,0:T(2,128)(2,1)}), bf16[8,2,7296]{2,1,0:T(2,128)(2,1)S(1)}, u32[]{:S(2)}, u32[]{:S(2)}) async-start(bf16[8,2,7296]{2,1,0:T(2,128)(2,1)} %pack.1), calls=%async_computation | async-start | bytes 466944 | tf_op jit(solution)/shard_map/all_to_all | solution.py:125
  17.5 1.9 %collective-permute-start = (bf16[16,7296]{1,0:T(8,128)(2,1)S(1)}, bf16[16,7296]{1,0:T(8,128)(2,1)S(1)}, u32[]{:S(2)}, u32[]{:S(2)}) collective-permute-start(bf16[16,7296]{1,0:T(8,128)(2,1)S(1)} %reshape.6.own_ref), channel_id=1, source_target_pairs={{0,8},{8,0},{1,9},{9,1},{2,10},{10,2},{3,11},{11,3},{4,12},{12,4},... | collective-permute-start | bytes 700424 | tf_op jit(solution)/shard_map/ppermute | solution.py:130
  23.7 1.7 %collective-permute-start.1 = (bf16[16,7168]{1,0:T(8,128)(2,1)S(1)}, bf16[16,7168]{1,0:T(8,128)(2,1)S(1)}, u32[]{:S(2)}, u32[]{:S(2)}) collective-permute-start(bf16[16,7168]{1,0:T(8,128)(2,1)S(1)} %get-tuple-element.20), channel_id=1, source_target_pairs={{0,8},{8,0},{1,9},{9,1},{2,10},{10,2},{3,11},{11,3},{4,12},{12,4},... | collective-permute-start | bytes 688136 | tf_op jit(solution)/shard_map/ppermute | solution.py:156

commit v3 on v1

v3 whole, which is shorter than its diff:
```python
import jax
import jax.numpy as jnp
from jax import lax
from jax.experimental import pallas as pl
from jax.experimental.pallas import tpu as pltpu
from jax.sharding import PartitionSpec as P

SPLIT = 8
LANES = 128
VMEM_LIMIT = 32 * 1024 * 1024
COLUMNS = 1024


def pack_kernel(tokens_ref, routes_ref, weights_ref, packed_ref):
    rows, width = tokens_ref.shape
    copies = packed_ref.shape[0]
    extra = packed_ref.shape[2] - width
    columns = lax.broadcasted_iota(jnp.int32, (rows, extra), 1)
    combine = jnp.zeros((rows, extra), jnp.float32)
    for k in range(routes_ref.shape[0]):
        route = jnp.concatenate([routes_ref[k : k + 1, r : r + 1] for r in range(rows)], axis=0)
        weight = weights_ref[:, k : k + 1].astype(jnp.float32)
        combine += jnp.where(columns == route, weight, 0.0)
    combine = combine.astype(jnp.bfloat16)
    for c in range(copies):
        packed_ref[c, :, :width] = tokens_ref[...]
        packed_ref[c, :, width:] = combine


def expert_kernel(own_ref, other_ref, gate_ref, up_ref, down_ref, own_out, other_out):
    devs, tok_rows, wide = own_ref.shape
    _, width, hidden_units = gate_ref.shape
    rows = devs * tok_rows

    def tokens_part(part):
        halves = [ref[:, :, part] for ref in (own_ref, other_ref)]
        return jnp.concatenate([half.reshape(rows, half.shape[2]) for half in halves], axis=0)

    expert = lax.axis_index("node") * (lax.axis_size("dev") // SPLIT) + lax.axis_index("dev") // SPLIT
    combine = tokens_part(slice(width, wide)).astype(jnp.float32)
    columns = lax.broadcasted_iota(jnp.int32, combine.shape, 1)
    scale = jnp.sum(jnp.where(columns == expert, combine, 0.0), axis=1, keepdims=True)
    gate = jnp.zeros((2 * rows, hidden_units), jnp.float32)
    upper = jnp.zeros((2 * rows, hidden_units), jnp.float32)
    for start in range(0, width, COLUMNS):
        part = slice(start, start + COLUMNS)
        block = tokens_part(part)
        gate += jnp.dot(block, gate_ref[0, part, :], preferred_element_type=jnp.float32)
        upper += jnp.dot(block, up_ref[0, part, :], preferred_element_type=jnp.float32)
    hidden = (gate / (1.0 + jnp.exp(-gate)) * upper).astype(jnp.bfloat16)
    for start in range(0, width, COLUMNS):
        part = slice(start, start + COLUMNS)
        output = scale * jnp.dot(
            hidden, down_ref[0, :, part], preferred_element_type=jnp.float32
        )
        own_out[:, :, part] = output[:rows].reshape(devs, tok_rows, COLUMNS)
        other = output[rows:].astype(jnp.bfloat16)
        other_out[:, :, part] = other.reshape(devs, tok_rows, COLUMNS)


def per_device(tokens, routes, route_weights, gate_weight, up_weight, down_weight):
    tok_rows, width = tokens.shape
    nodes = lax.axis_size("node")
    devs = lax.axis_size("dev")
    per_node = devs // SPLIT
    experts = nodes * per_node
    wide = width + -(-experts // LANES) * LANES
    vmem = pl.BlockSpec(memory_space=pltpu.VMEM)
    swap = [(i, i ^ 1) for i in range(nodes)]

    packed = pl.pallas_call(
        pack_kernel,
        out_shape=jax.ShapeDtypeStruct((devs, tok_rows, wide), jnp.bfloat16),
        in_specs=[vmem] * 3,
        out_specs=vmem,
        name="pack",
    )(tokens, routes.T, route_weights)
    here = [(i, i) for i in range(nodes)]
    packed, *weights = lax.optimization_barrier((packed, gate_weight, up_weight, down_weight))
    resident = [lax.ppermute(weight, "node", here) for weight in weights]
    own = lax.all_to_all(packed, "dev", split_axis=0, concat_axis=0, tiled=True)
    other = lax.ppermute(own, "node", swap)
    own_out, other_out = pl.pallas_call(
        expert_kernel,
        out_shape=(
            jax.ShapeDtypeStruct((devs, tok_rows, width), jnp.float32),
            jax.ShapeDtypeStruct((devs, tok_rows, width), jnp.bfloat16),
        ),
        in_specs=[vmem] * 5,
        out_specs=(vmem, vmem),
        compiler_params=pltpu.CompilerParams(vmem_limit_bytes=VMEM_LIMIT),
        name="expert",
    )(own, other, *resident)
    arrived = lax.ppermute(other_out, "node", swap)
    partial = (own_out + arrived.astype(jnp.float32)).astype(jnp.bfloat16)
    returned = lax.all_to_all(
        partial, "dev", split_axis=0, concat_axis=0, tiled=True
    )
    return jnp.sum(returned.astype(jnp.float32), axis=0).astype(jnp.bfloat16)


def solution(mesh):
    rows = P(("replica", "node", "dev"), None)
    shards = P(("node", "dev"), None, None)
    return jax.shard_map(
        per_device,
        mesh=mesh,
        in_specs=(rows, rows, rows, shards, shards, shards),
        out_specs=rows,
        check_vma=False,
    )
```

time: 42 us -> 42 us (level)
  starting transfers between devices: 0.27 us -> 6.32 us
  local copies, waits for them, and re-layouts: 3.51 us -> 0 us
  Pallas kernels: 6.45 us -> 3.68 us
    ppermute x0 -> x3, starting transfers between devices: none -> 6.12 us  [per_device(): resident = [lax.ppermute(weight, 'node', here) for weight in weights]]
    unnamed x3 -> x0, local copies, waits for them, and re-layouts: 3.33 us -> none
    pallas_call x1, Pallas kernels: 4.92 us -> 2.09 us  [per_device(): pl.pallas_call(expert_kernel, out_shape=(jax.ShapeDtypeStruct((devs, tok_...]
  transfers between devices with their start and end apart: 2 -> 5, of which waited for: 2 -> 2; matrix products, arithmetic and copies ran while one was open for 0% -> 0% of each run, Pallas kernels for 0% -> 0%
where the time goes in v3:
time: 42 us; the launch traced here: 41.6 us
  blocking collectives  27.7 us (66%)
  starting transfers between devices  6.32 us (15%)
  Pallas kernels  3.68 us (9%)
  waiting for transfers between devices  2.85 us (7%)
  other arithmetic  1.05 us (2%)
    all_to_all x1, blocking collectives, per_device(): own = lax.all_to_all(packed, 'dev', split_axis=0, concat_axis=0, tiled=True)  15.8 us
    all_to_all x1, blocking collectives, per_device(): lax.all_to_all(partial, 'dev', split_axis=0, concat_axis=0, tiled=True)  11.9 us
    ppermute x3, starting transfers between devices, per_device(): resident = [lax.ppermute(weight, 'node', here) for weight in weights]  6.12 us
    pallas_call x1, Pallas kernels, per_device(): pl.pallas_call(expert_kernel, out_shape=(jax.ShapeDtypeStruct((devs, tok_...  2.09 us
    pallas_call x1, Pallas kernels, per_device(): pl.pallas_call(pack_kernel, out_shape=jax.ShapeDtypeStruct((devs, tok_row...  1.59 us
    ppermute x1, waiting for transfers between devices, per_device(): other = lax.ppermute(own, 'node', swap)  1.49 us
    ppermute x1, waiting for transfers between devices, per_device(): arrived = lax.ppermute(other_out, 'node', swap)  1.35 us
  transfers between devices with their start and end apart: 5, of which 2 were waited for; matrix products, arithmetic and copies ran while one was open for 0% of the time, Pallas kernels for 0%

profile of v3, /device:TPU:0, one launch (start us, length us, event | category | flops | bytes accessed | tf_op | source)
XLA Modules:
  0.0 41.6 jit_solution(12886971490609332329)
XLA Ops:
  0.0 1.6 %pack.1 = bf16[8,2,7296]{2,1,0:T(2,128)(2,1)} custom-call(bf16[2,7168]{1,0:T(2,128)(2,1)} %tokens_ref.1, s32[1,2]{1,0:T(1,128)} %bitcast.1, bf16[2,1]{1,0:T(2,128)(2,1)} %weights_ref.1), custom_call_target="tpu_custom_call" | custom-call | tf_op jit(solution)/shard_map/pack/pallas_call | solution.py:71
  1.6 2.0 %collective-permute-start.1 = (bf16[1,7168,256]{2,1,0:T(8,128)(2,1)}, bf16[1,7168,256]{2,1,0:T(8,128)(2,1)S(1)}, u32[]{:S(2)}, u32[]{:S(2)}) collective-permute-start(bf16[1,7168,256]{2,1,0:T(8,128)(2,1)} %param.9), channel_id=1, source_target_pairs={{0,0},{8,8},{1,1},{9,9},{2,2},{10,10},{3,3},{11,11},{4,4},{12,12},... | collective-permute-start | bytes 11010056 | tf_op jit(solution)/shard_map/ppermute | solution.py:80
  3.6 2.0 %collective-permute-start.2 = (bf16[1,7168,256]{2,1,0:T(8,128)(2,1)}, bf16[1,7168,256]{2,1,0:T(8,128)(2,1)S(1)}, u32[]{:S(2)}, u32[]{:S(2)}) collective-permute-start(bf16[1,7168,256]{2,1,0:T(8,128)(2,1)} %param.10), channel_id=1, source_target_pairs={{0,0},{8,8},{1,1},{9,9},{2,2},{10,10},{3,3},{11,11},{4,4},{12,12},... | collective-permute-start | bytes 11010056 | tf_op jit(solution)/shard_map/ppermute | solution.py:80
  5.7 2.0 %collective-permute-start.3 = (bf16[1,256,7168]{2,1,0:T(8,128)(2,1)}, bf16[1,256,7168]{2,1,0:T(8,128)(2,1)S(1)}, u32[]{:S(2)}, u32[]{:S(2)}) collective-permute-start(bf16[1,256,7168]{2,1,0:T(8,128)(2,1)} %param.11), channel_id=1, source_target_pairs={{0,0},{8,8},{1,1},{9,9},{2,2},{10,10},{3,3},{11,11},{4,4},{12,12},... | collective-permute-start | bytes 11010056 | tf_op jit(solution)/shard_map/ppermute | solution.py:80
  7.7 15.8 %all_to_all.10.own_ref = bf16[8,2,7296]{2,1,0:T(2,128)(2,1)S(1)} all-to-all(bf16[8,2,7296]{2,1,0:T(2,128)(2,1)} %pack.1), channel_id=1, replica_groups=mesh['replica'=2,'node'=2,'dev'=8] {'dev'}, dimensions={0} | all-to-all | bytes 466944 | tf_op jit(solution)/shard_map/all_to_all | solution.py:81
  23.5 0.0 collective-permute-start
  23.5 1.5 %collective-permute-done.other_ref = bf16[8,2,7296]{2,1,0:T(2,128)(2,1)S(1)} collective-permute-done((bf16[8,2,7296]{2,1,0:T(2,128)(2,1)S(1)}, bf16[8,2,7296]{2,1,0:T(2,128)(2,1)S(1)}, u32[]{:S(2)}, u32[]{:S(2)}) %collective-permute-start) | collective-permute-done | bytes 233504 | tf_op jit(solution)/shard_map/ppermute | solution.py:82
  25.0 0.0 collective-permute-done.1.gate_ref
  25.0 0.0 collective-permute-done.2.up_ref
  25.0 0.0 collective-permute-done.3.down_ref
  25.0 2.1 %expert.1 = (f32[8,2,7168]{2,1,0:T(2,128)S(1)}, bf16[8,2,7168]{2,1,0:T(2,128)(2,1)S(1)}) custom-call(bf16[8,2,7296]{2,1,0:T(2,128)(2,1)S(1)} %all_to_all.10.own_ref, bf16[8,2,7296]{2,1,0:T(2,128)(2,1)S(1)} %collective-permute-done.other_ref, bf16[1,7168,256]{2,1,0:T(8,128)(2,1)S(1)} %collective-permute-done.1.gate_ref, ...), custom_call_target="tpu_custom_call" | custom-call | tf_op jit(solution)/shard_map/expert/pallas_call | solution.py:83
  27.1 0.2 collective-permute-start.4
  27.3 1.4 %collective-permute-done.4 = bf16[8,2,7168]{2,1,0:T(2,128)(2,1)S(1)} collective-permute-done((bf16[8,2,7168]{2,1,0:T(2,128)(2,1)S(1)}, bf16[8,2,7168]{2,1,0:T(2,128)(2,1)S(1)}, u32[]{:S(2)}, u32[]{:S(2)}) %collective-permute-start.4) | collective-permute-done | bytes 229408 | tf_op jit(solution)/shard_map/ppermute | solution.py:94
  28.6 0.2 add_convert_fusion
  28.9 11.9 %all_to_all.11 = bf16[8,2,7168]{2,1,0:T(2,128)(2,1)S(1)} all-to-all(bf16[8,2,7168]{2,1,0:T(2,128)(2,1)S(1)} %add_convert_fusion), channel_id=1, replica_groups=mesh['replica'=2,'node'=2,'dev'=8] {'dev'}, dimensions={0} | all-to-all | bytes 458752 | tf_op jit(solution)/shard_map/all_to_all | solution.py:96
  40.8 0.8 %reduce_sum.12 = bf16[2,7168]{1,0:T(2,128)(2,1)} reduce(bf16[8,2,7168]{2,1,0:T(2,128)(2,1)S(1)} %all_to_all.11, bf16[]{:T(256)} %constant.2.clone.1), dimensions={0}, to_apply=%region_0.0 | reduce | flops 100352 | bytes 258050 | tf_op jit(solution)/shard_map/reduce_sum | solution.py:99
Async XLA Ops:
  1.6 23.4 %collective-permute-start.1 = (bf16[1,7168,256]{2,1,0:T(8,128)(2,1)}, bf16[1,7168,256]{2,1,0:T(8,128)(2,1)S(1)}, u32[]{:S(2)}, u32[]{:S(2)}) collective-permute-start(bf16[1,7168,256]{2,1,0:T(8,128)(2,1)} %param.9), channel_id=1, source_target_pairs={{0,0},{8,8},{1,1},{9,9},{2,2},{10,10},{3,3},{11,11},{4,4},{12,12},... | collective-permute-start | bytes 11010056 | tf_op jit(solution)/shard_map/ppermute | solution.py:80
  3.6 21.4 %collective-permute-start.2 = (bf16[1,7168,256]{2,1,0:T(8,128)(2,1)}, bf16[1,7168,256]{2,1,0:T(8,128)(2,1)S(1)}, u32[]{:S(2)}, u32[]{:S(2)}) collective-permute-start(bf16[1,7168,256]{2,1,0:T(8,128)(2,1)} %param.10), channel_id=1, source_target_pairs={{0,0},{8,8},{1,1},{9,9},{2,2},{10,10},{3,3},{11,11},{4,4},{12,12},... | collective-permute-start | bytes 11010056 | tf_op jit(solution)/shard_map/ppermute | solution.py:80
  5.7 19.3 %collective-permute-start.3 = (bf16[1,256,7168]{2,1,0:T(8,128)(2,1)}, bf16[1,256,7168]{2,1,0:T(8,128)(2,1)S(1)}, u32[]{:S(2)}, u32[]{:S(2)}) collective-permute-start(bf16[1,256,7168]{2,1,0:T(8,128)(2,1)} %param.11), channel_id=1, source_target_pairs={{0,0},{8,8},{1,1},{9,9},{2,2},{10,10},{3,3},{11,11},{4,4},{12,12},... | collective-permute-start | bytes 11010056 | tf_op jit(solution)/shard_map/ppermute | solution.py:80
  23.5 1.5 %collective-permute-start = (bf16[8,2,7296]{2,1,0:T(2,128)(2,1)S(1)}, bf16[8,2,7296]{2,1,0:T(2,128)(2,1)S(1)}, u32[]{:S(2)}, u32[]{:S(2)}) collective-permute-start(bf16[8,2,7296]{2,1,0:T(2,128)(2,1)S(1)} %all_to_all.10.own_ref), channel_id=1, source_target_pairs={{0,8},{8,0},{1,9},{9,1},{2,10},{10,2},{3,11},{11,3},{4,12},{12,4},... | collective-permute-start | bytes 700424 | tf_op jit(solution)/shard_map/ppermute | solution.py:82
  27.1 1.6 %collective-permute-start.4 = (bf16[8,2,7168]{2,1,0:T(2,128)(2,1)S(1)}, bf16[8,2,7168]{2,1,0:T(2,128)(2,1)S(1)}, u32[]{:S(2)}, u32[]{:S(2)}) collective-permute-start(bf16[8,2,7168]{2,1,0:T(2,128)(2,1)S(1)} %get-tuple-element.16), channel_id=1, source_target_pairs={{0,8},{8,0},{1,9},{9,1},{2,10},{10,2},{3,11},{11,3},{4,12},{12,4},... | collective-permute-start | bytes 688136 | tf_op jit(solution)/shard_map/ppermute | solution.py:94

commit v4 on v3

v4 whole, which is shorter than its diff:
```python
import jax
import jax.numpy as jnp
from jax import lax
from jax.experimental import pallas as pl
from jax.experimental.pallas import tpu as pltpu
from jax.sharding import PartitionSpec as P

SPLIT = 8
LANES = 128
VMEM_ROOM = 52 * 1024 * 1024
EXPERT_LIMIT = 24 * 1024 * 1024
COLUMNS = 1024


def pack_kernel(tokens_ref, routes_ref, weights_ref, packed_ref):
    rows, width = tokens_ref.shape
    copies = packed_ref.shape[0]
    extra = packed_ref.shape[2] - width
    columns = lax.broadcasted_iota(jnp.int32, (rows, extra), 1)
    combine = jnp.zeros((rows, extra), jnp.float32)
    for k in range(routes_ref.shape[0]):
        route = jnp.concatenate([routes_ref[k : k + 1, r : r + 1] for r in range(rows)], axis=0)
        weight = weights_ref[:, k : k + 1].astype(jnp.float32)
        combine += jnp.where(columns == route, weight, 0.0)
    combine = combine.astype(jnp.bfloat16)
    for c in range(copies):
        packed_ref[c, :, :width] = tokens_ref[...]
        packed_ref[c, :, width:] = combine


def load_kernel(weight_hbm, held_ref, sem):
    copy = pltpu.make_async_copy(weight_hbm, held_ref, sem)
    copy.start()
    copy.wait()


def load(weight, held):
    return pl.pallas_call(
        load_kernel,
        out_shape=pltpu.VMEM(weight.shape, weight.dtype),
        in_specs=[pl.BlockSpec(memory_space=pltpu.HBM)],
        out_specs=pl.BlockSpec(memory_space=pltpu.VMEM),
        scratch_shapes=[pltpu.SemaphoreType.DMA],
        compiler_params=pltpu.CompilerParams(vmem_limit_bytes=VMEM_ROOM - held),
        cost_estimate=pl.CostEstimate(
            flops=0, transcendentals=0, bytes_accessed=2 * weight.size
        ),
        name="load",
    )(weight)


def expert_kernel(
    near_ref, far_ref, near_other_ref, far_other_ref, gate_ref, up_ref, down_ref,
    own_out, other_out,
):
    groups, tok_rows, wide = near_ref.shape
    _, width, hidden_units = gate_ref.shape
    rows = groups * tok_rows
    refs = (near_ref, far_ref, near_other_ref, far_other_ref)

    def tokens_part(part):
        pieces = [ref[:, :, part] for ref in refs]
        return jnp.concatenate([piece.reshape(rows, piece.shape[2]) for piece in pieces], axis=0)

    dev = lax.axis_index("dev")
    expert = lax.axis_index("node") * (lax.axis_size("dev") // SPLIT) + dev // SPLIT
    side = dev % 2
    combine = tokens_part(slice(width, wide)).astype(jnp.float32)
    columns = lax.broadcasted_iota(jnp.int32, combine.shape, 1)
    scale = jnp.sum(jnp.where(columns == expert, combine, 0.0), axis=1, keepdims=True)
    gate = jnp.zeros((4 * rows, hidden_units), jnp.float32)
    upper = jnp.zeros((4 * rows, hidden_units), jnp.float32)
    for start in range(0, width, COLUMNS):
        part = slice(start, start + COLUMNS)
        block = tokens_part(part)
        gate += jnp.dot(block, gate_ref[0, part, :], preferred_element_type=jnp.float32)
        upper += jnp.dot(block, up_ref[0, part, :], preferred_element_type=jnp.float32)
    hidden = (gate / (1.0 + jnp.exp(-gate)) * upper).astype(jnp.bfloat16)
    for start in range(0, width, COLUMNS):
        part = slice(start, start + COLUMNS)
        output = scale * jnp.dot(
            hidden, down_ref[0, :, part], preferred_element_type=jnp.float32
        )
        shape = (groups, tok_rows, COLUMNS)
        own_out[:, side, :, part] = output[:rows].reshape(shape)
        own_out[:, 1 - side, :, part] = output[rows : 2 * rows].reshape(shape)
        other = output[2 * rows :].astype(jnp.bfloat16)
        other_out[:, side, :, part] = other[:rows].reshape(shape)
        other_out[:, 1 - side, :, part] = other[rows:].reshape(shape)


def per_device(tokens, routes, route_weights, gate_weight, up_weight, down_weight):
    tok_rows, width = tokens.shape
    nodes = lax.axis_size("node")
    devs = lax.axis_size("dev")
    groups = devs // 2
    experts = nodes * (devs // SPLIT)
    wide = width + -(-experts // LANES) * LANES
    vmem = pl.BlockSpec(memory_space=pltpu.VMEM)
    swap = [(i, i ^ 1) for i in range(nodes)]
    beside = [(i, i ^ 1) for i in range(devs)]
    lines = [list(range(side, devs, 2)) for side in range(2)]

    packed = pl.pallas_call(
        pack_kernel,
        out_shape=pltpu.VMEM((groups, tok_rows, wide), jnp.bfloat16),
        in_specs=[vmem] * 3,
        out_specs=vmem,
        name="pack",
    )(tokens, routes.T, route_weights)
    near = lax.all_to_all(
        packed, "dev", split_axis=0, concat_axis=0, tiled=True, axis_index_groups=lines
    )
    near, gate_source, up_source = lax.optimization_barrier((near, gate_weight, up_weight))
    far = lax.ppermute(near, "dev", beside)
    near_other = lax.ppermute(near, "node", swap)
    piece = 2 * groups * tok_rows * wide
    weight_bytes = 2 * gate_weight.size
    gate_held = load(gate_source, 3 * piece + weight_bytes)
    up_held = load(up_source, 3 * piece + 2 * weight_bytes)
    far, near_other, gate_held, up_held, down_source = lax.optimization_barrier(
        (far, near_other, gate_held, up_held, down_weight)
    )
    far_other = lax.ppermute(far, "node", swap)
    down_held = load(down_source, 4 * piece + 3 * weight_bytes)
    shape = (groups, 2, tok_rows, width)
    own_out, other_out = pl.pallas_call(
        expert_kernel,
        out_shape=(
            jax.ShapeDtypeStruct(shape, jnp.float32),
            jax.ShapeDtypeStruct(shape, jnp.bfloat16),
        ),
        in_specs=[vmem] * 7,
        out_specs=(vmem, vmem),
        compiler_params=pltpu.CompilerParams(vmem_limit_bytes=EXPERT_LIMIT),
        name="expert",
    )(near, far, near_other, far_other, gate_held, up_held, down_held)
    arrived = lax.ppermute(other_out, "node", swap)
    partial = (own_out + arrived.astype(jnp.float32)).astype(jnp.bfloat16)
    returned = lax.all_to_all(
        partial.reshape(devs, tok_rows, width), "dev", split_axis=0, concat_axis=0, tiled=True
    )
    return jnp.sum(returned.astype(jnp.float32), axis=0).astype(jnp.bfloat16)


def solution(mesh):
    rows = P(("replica", "node", "dev"), None)
    shards = P(("node", "dev"), None, None)
    return jax.shard_map(
        per_device,
        mesh=mesh,
        in_specs=(rows, rows, rows, shards, shards, shards),
        out_specs=rows,
        check_vma=False,
    )
```

time: 42 us -> 37 us (0.88)
  starting transfers between devices: 6.32 us -> 1.74 us
  blocking collectives: 27.7 us -> 24.1 us
  Pallas kernels: 3.68 us -> 5.56 us
  waiting for transfers between devices: 2.85 us -> 4.12 us
    ppermute x4 -> x3, starting transfers between devices: 6.12 us -> 1.53 us  [the longest x1 1.52 us: per_device(): far = lax.ppermute(near, 'dev', beside)]
    all_to_all x2, blocking collectives: 27.7 us -> 24.1 us  [the longest x1 12.1 us: per_device(): lax.all_to_all(partial.reshape(devs, tok_rows, width), 'dev', split_axis=...]
    pallas_call x2 -> x5, Pallas kernels: 3.68 us -> 5.56 us  [the longest x3 2.56 us: load(): pl.pallas_call(load_kernel, out_shape=pltpu.VMEM(weight.shape, weight.dty...]
    ppermute x4 -> x3, waiting for transfers between devices: 1.5 us -> 2.78 us  [the longest x1 1.73 us: per_device(): far = lax.ppermute(near, 'dev', beside)]
  transfers between devices with their start and end apart: 5 -> 4, of which waited for: 2 -> 3; matrix products, arithmetic and copies ran while one was open for 0% -> 0% of each run, Pallas kernels for 0% -> 7%
where the time goes in v4:
time: 37 us; the launch traced here: 36.7 us
  blocking collectives  24.1 us (65%)
  Pallas kernels  5.56 us (15%)
  waiting for transfers between devices  4.12 us (11%)
  starting transfers between devices  1.74 us (5%)
  other arithmetic  1.05 us (3%)
    all_to_all x1, blocking collectives, per_device(): lax.all_to_all(partial.reshape(devs, tok_rows, width), 'dev', split_axis=...  12.1 us
    all_to_all x1, blocking collectives, per_device(): lax.all_to_all(packed, 'dev', split_axis=0, concat_axis=0, tiled=True, ax...  12 us
    pallas_call x3, Pallas kernels, load(): pl.pallas_call(load_kernel, out_shape=pltpu.VMEM(weight.shape, weight.dty...  2.56 us
    pallas_call x1, Pallas kernels, per_device(): pl.pallas_call(expert_kernel, out_shape=(jax.ShapeDtypeStruct(shape, jnp....  2.09 us
    ppermute x1, waiting for transfers between devices, per_device(): far = lax.ppermute(near, 'dev', beside)  1.73 us
    ppermute x1, starting transfers between devices, per_device(): far = lax.ppermute(near, 'dev', beside)  1.52 us
    ppermute x1, waiting for transfers between devices, per_device(): arrived = lax.ppermute(other_out, 'node', swap)  1.34 us
    ppermute x1, waiting for transfers between devices, per_device(): far_other = lax.ppermute(far, 'node', swap)  1.04 us
  transfers between devices with their start and end apart: 4, of which 3 were waited for; matrix products, arithmetic and copies ran while one was open for 0% of the time, Pallas kernels for 7%

profile of v4, /device:TPU:0, one launch (start us, length us, event | category | flops | bytes accessed | tf_op | source)
XLA Modules:
  0.0 36.7 jit_solution(12267077855910853057)
XLA Ops:
  0.0 0.9 %pack.1 = bf16[4,2,7296]{2,1,0:T(2,128)(2,1)S(1)} custom-call(bf16[2,7168]{1,0:T(2,128)(2,1)} %tokens_ref.1, s32[1,2]{1,0:T(1,128)} %bitcast.3, bf16[2,1]{1,0:T(2,128)(2,1)} %weights_ref.1), custom_call_target="tpu_custom_call" | custom-call | tf_op jit(solution)/shard_map/pack/pallas_call | solution.py:104
  0.9 12.0 %all_to_all.10.near_ref = bf16[4,2,7296]{2,1,0:T(2,128)(2,1)S(1)} all-to-all(bf16[4,2,7296]{2,1,0:T(2,128)(2,1)S(1)} %pack.1), channel_id=1, replica_groups={{0,2,4,6},{1,3,5,7},{8,10,12,14},{9,11,13,15},{16,18,20,22},{17,19,21,2..., dimensions={0} | all-to-all | bytes 233472 | tf_op jit(solution)/shard_map/all_to_all | solution.py:111
  12.9 0.0 copy-start
  12.9 0.0 collective-permute-start.1
  12.9 1.5 %collective-permute-start = (bf16[4,2,7296]{2,1,0:T(2,128)(2,1)S(1)}, bf16[4,2,7296]{2,1,0:T(2,128)(2,1)S(1)}, u32[]{:S(2)}, u32[]{:S(2)}) collective-permute-start(bf16[4,2,7296]{2,1,0:T(2,128)(2,1)S(1)} %all_to_all.10.near_ref), channel_id=1, source_target_pairs={{0,1},{1,0},{2,3},{3,2},{4,5},{5,4},{6,7},{7,6},{8,9},{9,8},{10,11... | collective-permute-start | bytes 350216 | tf_op jit(solution)/shard_map/ppermute | solution.py:115
  14.5 2.0 %load.3.gate_ref = bf16[1,7168,256]{2,1,0:T(8,128)(2,1)S(1)} custom-call(bf16[1,7168,256]{2,1,0:T(8,128)(2,1)} %weight_hbm), custom_call_target="tpu_custom_call" | custom-call | bytes 3670016 | tf_op jit(solution)/shard_map/load/pallas_call | solution.py:38
  16.5 0.0 copy-done
  16.5 0.0 copy-start.1
  16.5 0.3 load.4.up_ref
  16.8 0.0 collective-permute-done.1.near_other_ref
  16.8 1.7 %collective-permute-done.far_ref = bf16[4,2,7296]{2,1,0:T(2,128)(2,1)S(1)} collective-permute-done((bf16[4,2,7296]{2,1,0:T(2,128)(2,1)S(1)}, bf16[4,2,7296]{2,1,0:T(2,128)(2,1)S(1)}, u32[]{:S(2)}, u32[]{:S(2)}) %collective-permute-start) | collective-permute-done | bytes 116768 | tf_op jit(solution)/shard_map/ppermute | solution.py:115
  18.5 0.0 collective-permute-start.2
  18.5 0.0 copy-done.1
  18.6 0.3 load.5.down_ref
  18.8 1.0 %collective-permute-done.2.far_other_ref = bf16[4,2,7296]{2,1,0:T(2,128)(2,1)S(1)} collective-permute-done((bf16[4,2,7296]{2,1,0:T(2,128)(2,1)S(1)}, bf16[4,2,7296]{2,1,0:T(2,128)(2,1)S(1)}, u32[]{:S(2)}, u32[]{:S(2)}) %collective-permute-start.2) | collective-permute-done | bytes 116768 | tf_op jit(solution)/shard_map/ppermute | solution.py:124
  19.9 2.1 %expert.1 = (f32[4,2,2,7168]{3,2,1,0:T(2,128)S(1)}, bf16[4,2,2,7168]{3,2,1,0:T(2,128)(2,1)S(1)}) custom-call(bf16[4,2,7296]{2,1,0:T(2,128)(2,1)S(1)} %all_to_all.10.near_ref, bf16[4,2,7296]{2,1,0:T(2,128)(2,1)S(1)} %collective-permute-done.far_ref, bf16[4,2,7296]{2,1,0:T(2,128)(2,1)S(1)} %collective-permute-done.1.near_other_ref, ...), custom_call_target="tpu_custom_call" | custom-call | tf_op jit(solution)/shard_map/expert/pallas_call | solution.py:127
  22.0 0.2 collective-permute-start.3
  22.2 1.3 %collective-permute-done.3 = bf16[4,2,2,7168]{3,2,1,0:T(2,128)(2,1)S(1)} collective-permute-done((bf16[4,2,2,7168]{3,2,1,0:T(2,128)(2,1)S(1)}, bf16[4,2,2,7168]{3,2,1,0:T(2,128)(2,1)S(1)}, u32[]{:S(2)}, u32[]{:S(2)}) %collective-permute-start.3) | collective-permute-done | bytes 229408 | tf_op jit(solution)/shard_map/ppermute | solution.py:138
  23.5 0.2 add_convert_fusion
  23.8 12.1 %all_to_all.11 = bf16[8,2,7168]{2,1,0:T(2,128)(2,1)S(1)} all-to-all(bf16[8,2,7168]{2,1,0:T(2,128)(2,1)S(1)} %bitcast.2), channel_id=1, replica_groups=mesh['replica'=2,'node'=2,'dev'=8] {'dev'}, dimensions={0} | all-to-all | bytes 458752 | tf_op jit(solution)/shard_map/all_to_all | solution.py:140
  35.8 0.8 %reduce_sum.12 = bf16[2,7168]{1,0:T(2,128)(2,1)} reduce(bf16[8,2,7168]{2,1,0:T(2,128)(2,1)S(1)} %all_to_all.11, bf16[]{:T(256)} %constant.2.clone.1), dimensions={0}, to_apply=%region_0.0 | reduce | flops 100352 | bytes 258050 | tf_op jit(solution)/shard_map/reduce_sum | solution.py:143
Async XLA Ops:
  12.9 3.6 %copy-start = (bf16[1,7168,256]{2,1,0:T(8,128)(2,1)S(1)}, bf16[1,7168,256]{2,1,0:T(8,128)(2,1)}, u32[]{:S(2)}) copy-start(bf16[1,7168,256]{2,1,0:T(8,128)(2,1)} %weight_hbm.1) | copy-start | bytes 11010052
  12.9 3.9 %collective-permute-start.1 = (bf16[4,2,7296]{2,1,0:T(2,128)(2,1)S(1)}, bf16[4,2,7296]{2,1,0:T(2,128)(2,1)S(1)}, u32[]{:S(2)}, u32[]{:S(2)}) collective-permute-start(bf16[4,2,7296]{2,1,0:T(2,128)(2,1)S(1)} %all_to_all.10.near_ref), channel_id=1, source_target_pairs={{0,8},{8,0},{1,9},{9,1},{2,10},{10,2},{3,11},{11,3},{4,12},{12,4},... | collective-permute-start | bytes 350216 | tf_op jit(solution)/shard_map/ppermute | solution.py:116
  12.9 5.6 %collective-permute-start = (bf16[4,2,7296]{2,1,0:T(2,128)(2,1)S(1)}, bf16[4,2,7296]{2,1,0:T(2,128)(2,1)S(1)}, u32[]{:S(2)}, u32[]{:S(2)}) collective-permute-start(bf16[4,2,7296]{2,1,0:T(2,128)(2,1)S(1)} %all_to_all.10.near_ref), channel_id=1, source_target_pairs={{0,1},{1,0},{2,3},{3,2},{4,5},{5,4},{6,7},{7,6},{8,9},{9,8},{10,11... | collective-permute-start | bytes 350216 | tf_op jit(solution)/shard_map/ppermute | solution.py:115
  16.5 2.0 %copy-start.1 = (bf16[1,256,7168]{2,1,0:T(8,128)(2,1)S(1)}, bf16[1,256,7168]{2,1,0:T(8,128)(2,1)}, u32[]{:S(2)}) copy-start(bf16[1,256,7168]{2,1,0:T(8,128)(2,1)} %weight_hbm.2) | copy-start | bytes 11010052
  18.5 1.3 %collective-permute-start.2 = (bf16[4,2,7296]{2,1,0:T(2,128)(2,1)S(1)}, bf16[4,2,7296]{2,1,0:T(2,128)(2,1)S(1)}, u32[]{:S(2)}, u32[]{:S(2)}) collective-permute-start(bf16[4,2,7296]{2,1,0:T(2,128)(2,1)S(1)} %collective-permute-done.far_ref), channel_id=1, source_target_pairs={{0,8},{8,0},{1,9},{9,1},{2,10},{10,2},{3,11},{11,3},{4,12},{12,4},... | collective-permute-start | bytes 350216 | tf_op jit(solution)/shard_map/ppermute | solution.py:124
  22.0 1.6 %collective-permute-start.3 = (bf16[4,2,2,7168]{3,2,1,0:T(2,128)(2,1)S(1)}, bf16[4,2,2,7168]{3,2,1,0:T(2,128)(2,1)S(1)}, u32[]{:S(2)}, u32[]{:S(2)}) collective-permute-start(bf16[4,2,2,7168]{3,2,1,0:T(2,128)(2,1)S(1)} %get-tuple-element.24), channel_id=1, source_target_pairs={{0,8},{8,0},{1,9},{9,1},{2,10},{10,2},{3,11},{11,3},{4,12},{12,4},... | collective-permute-start | bytes 688136 | tf_op jit(solution)/shard_map/ppermute | solution.py:138

commit v5 on v3

--- a/solution.py
+++ b/solution.py
@@ -8,10 +8,12 @@
 SPLIT = 8
 LANES = 128
 VMEM_LIMIT = 32 * 1024 * 1024
+SPARE = 2048
+SPACER_LIMIT = 38 * 1024 * 1024
 COLUMNS = 1024
 
 
-def pack_kernel(tokens_ref, routes_ref, weights_ref, packed_ref):
+def pack_kernel(tokens_ref, routes_ref, weights_ref, packed_ref, spare_ref):
     rows, width = tokens_ref.shape
     copies = packed_ref.shape[0]
     extra = packed_ref.shape[2] - width
@@ -27,7 +29,11 @@
         packed_ref[c, :, width:] = combine
 
 
-def expert_kernel(own_ref, other_ref, gate_ref, up_ref, down_ref, own_out, other_out):
+def spacer_kernel(packed_ref, spare_hbm, mark_ref):
+    mark_ref[...] = jnp.zeros_like(mark_ref)
+
+
+def expert_kernel(own_ref, other_ref, gate_ref, up_ref, down_ref, mark_ref, own_out, other_out):
     devs, tok_rows, wide = own_ref.shape
     _, width, hidden_units = gate_ref.shape
     rows = devs * tok_rows
@@ -68,16 +74,25 @@
     vmem = pl.BlockSpec(memory_space=pltpu.VMEM)
     swap = [(i, i ^ 1) for i in range(nodes)]
 
-    packed = pl.pallas_call(
+    packed, spare = pl.pallas_call(
         pack_kernel,
-        out_shape=jax.ShapeDtypeStruct((devs, tok_rows, wide), jnp.bfloat16),
+        out_shape=(
+            pltpu.VMEM((devs, tok_rows, wide), jnp.bfloat16),
+            jax.ShapeDtypeStruct((SPARE, width), jnp.bfloat16),
+        ),
         in_specs=[vmem] * 3,
-        out_specs=vmem,
+        out_specs=(vmem, pl.BlockSpec(memory_space=pltpu.HBM)),
         name="pack",
     )(tokens, routes.T, route_weights)
-    here = [(i, i) for i in range(nodes)]
-    packed, *weights = lax.optimization_barrier((packed, gate_weight, up_weight, down_weight))
-    resident = [lax.ppermute(weight, "node", here) for weight in weights]
+    mark = pl.pallas_call(
+        spacer_kernel,
+        out_shape=pltpu.VMEM((8, LANES), jnp.float32),
+        in_specs=[vmem, pl.BlockSpec(memory_space=pltpu.HBM)],
+        out_specs=vmem,
+        compiler_params=pltpu.CompilerParams(vmem_limit_bytes=SPACER_LIMIT),
+        name="spacer",
+    )(packed, spare)
+    packed, mark = lax.optimization_barrier((packed, mark))
     own = lax.all_to_all(packed, "dev", split_axis=0, concat_axis=0, tiled=True)
     other = lax.ppermute(own, "node", swap)
     own_out, other_out = pl.pallas_call(
@@ -86,16 +101,14 @@
             jax.ShapeDtypeStruct((devs, tok_rows, width), jnp.float32),
             jax.ShapeDtypeStruct((devs, tok_rows, width), jnp.bfloat16),
         ),
-        in_specs=[vmem] * 5,
+        in_specs=[vmem] * 6,
         out_specs=(vmem, vmem),
         compiler_params=pltpu.CompilerParams(vmem_limit_bytes=VMEM_LIMIT),
         name="expert",
-    )(own, other, *resident)
+    )(own, other, gate_weight, up_weight, down_weight, mark)
     arrived = lax.ppermute(other_out, "node", swap)
     partial = (own_out + arrived.astype(jnp.float32)).astype(jnp.bfloat16)
-    returned = lax.all_to_all(
-        partial, "dev", split_axis=0, concat_axis=0, tiled=True
-    )
+    returned = lax.all_to_all(partial, "dev", split_axis=0, concat_axis=0, tiled=True)
     return jnp.sum(returned.astype(jnp.float32), axis=0).astype(jnp.bfloat16)
 
 

time: 42 us -> 35.1 us (0.84)
  starting transfers between devices: 6.32 us -> 0.2 us
  Pallas kernels: 3.68 us -> 3 us
    ppermute x3 -> x0, starting transfers between devices: 6.12 us -> none  [per_device(): resident = [lax.ppermute(weight, 'node', here) for weight in weights]]
    pallas_call x1 -> x2, Pallas kernels: 1.59 us -> 0.91 us  [the longest x1 0.91 us: per_device(): pl.pallas_call(pack_kernel, out_shape=(pltpu.VMEM((devs, tok_rows, wide),...]
  transfers between devices with their start and end apart: 5 -> 2, of which waited for: 2 -> 2; matrix products, arithmetic and copies ran while one was open for 0% -> 0% of each run, Pallas kernels for 0% -> 0%
where the time goes in v5:
time: 35.1 us; the launch traced here: 34.9 us
  blocking collectives  27.8 us (79%)
  Pallas kernels  3 us (9%)
  waiting for transfers between devices  2.85 us (8%)
  other arithmetic  1.07 us (3%)
    all_to_all x1, blocking collectives, per_device(): own = lax.all_to_all(packed, 'dev', split_axis=0, concat_axis=0, tiled=True)  15.8 us
    all_to_all x1, blocking collectives, per_device(): lax.all_to_all(partial, 'dev', split_axis=0, concat_axis=0, tiled=True)  11.9 us
    pallas_call x1, Pallas kernels, per_device(): pl.pallas_call(expert_kernel, out_shape=(jax.ShapeDtypeStruct((devs, tok_...  2.09 us
    ppermute x1, waiting for transfers between devices, per_device(): other = lax.ppermute(own, 'node', swap)  1.49 us
    ppermute x1, waiting for transfers between devices, per_device(): arrived = lax.ppermute(other_out, 'node', swap)  1.35 us
    pallas_call x1, Pallas kernels, per_device(): pl.pallas_call(pack_kernel, out_shape=(pltpu.VMEM((devs, tok_rows, wide),...  0.91 us
    reduce_sum x1, other arithmetic, per_device(): return jnp.sum(returned.astype(jnp.float32), axis=0).astype(jnp.bfloat16)  0.82 us
  transfers between devices with their start and end apart: 2, of which 2 were waited for; matrix products, arithmetic and copies ran while one was open for 0% of the time, Pallas kernels for 0%

profile of v5, /device:TPU:0, one launch (start us, length us, event | category | flops | bytes accessed | tf_op | source)
XLA Modules:
  0.0 34.9 jit_solution(4819501782229303690)
XLA Ops:
  0.0 0.9 %pack.1 = (bf16[8,2,7296]{2,1,0:T(2,128)(2,1)S(1)}, bf16[2048,7168]{1,0:T(8,128)(2,1)}) custom-call(bf16[2,7168]{1,0:T(2,128)(2,1)} %tokens_ref.1, s32[1,2]{1,0:T(1,128)} %bitcast.1, bf16[2,1]{1,0:T(2,128)(2,1)} %weights_ref.1), custom_call_target="tpu_custom_call" | custom-call | tf_op jit(solution)/shard_map/pack/pallas_call | solution.py:77
  0.9 0.0 copy-start
  0.9 0.0 copy-start.1
  0.9 0.0 copy-start.2
  0.9 15.8 %all_to_all.10.own_ref = bf16[8,2,7296]{2,1,0:T(2,128)(2,1)S(1)} all-to-all(bf16[8,2,7296]{2,1,0:T(2,128)(2,1)S(1)} %get-tuple-element.13.packed_ref), channel_id=1, replica_groups=mesh['replica'=2,'node'=2,'dev'=8] {'dev'}, dimensions={0} | all-to-all | bytes 466944 | tf_op jit(solution)/shard_map/all_to_all | solution.py:96
  16.8 0.0 collective-permute-start
  16.8 1.5 %collective-permute-done.other_ref = bf16[8,2,7296]{2,1,0:T(2,128)(2,1)S(1)} collective-permute-done((bf16[8,2,7296]{2,1,0:T(2,128)(2,1)S(1)}, bf16[8,2,7296]{2,1,0:T(2,128)(2,1)S(1)}, u32[]{:S(2)}, u32[]{:S(2)}) %collective-permute-start) | collective-permute-done | bytes 233504 | tf_op jit(solution)/shard_map/ppermute | solution.py:97
  18.3 0.0 copy-done
  18.3 0.0 copy-done.1
  18.3 0.0 copy-done.2
  18.3 2.1 %expert.1 = (f32[8,2,7168]{2,1,0:T(2,128)S(1)}, bf16[8,2,7168]{2,1,0:T(2,128)(2,1)S(1)}) custom-call(bf16[8,2,7296]{2,1,0:T(2,128)(2,1)S(1)} %all_to_all.10.own_ref, bf16[8,2,7296]{2,1,0:T(2,128)(2,1)S(1)} %collective-permute-done.other_ref, bf16[1,7168,256]{2,1,0:T(8,128)(2,1)S(1)} %copy-done, bf16[1,7168,256]{2,1,0:T(8,128)(2,1)S(1)} %copy-done.1, ...), custom_call_target="tpu_custom_call" | custom-call | tf_op jit(solution)/shard_map/expert/pallas_call | solution.py:98
  20.4 0.2 collective-permute-start.1
  20.6 1.4 %collective-permute-done.1 = bf16[8,2,7168]{2,1,0:T(2,128)(2,1)S(1)} collective-permute-done((bf16[8,2,7168]{2,1,0:T(2,128)(2,1)S(1)}, bf16[8,2,7168]{2,1,0:T(2,128)(2,1)S(1)}, u32[]{:S(2)}, u32[]{:S(2)}) %collective-permute-start.1) | collective-permute-done | bytes 229408 | tf_op jit(solution)/shard_map/ppermute | solution.py:109
  21.9 0.3 add_convert_fusion
  22.2 11.9 %all_to_all.11 = bf16[8,2,7168]{2,1,0:T(2,128)(2,1)S(1)} all-to-all(bf16[8,2,7168]{2,1,0:T(2,128)(2,1)S(1)} %add_convert_fusion), channel_id=1, replica_groups=mesh['replica'=2,'node'=2,'dev'=8] {'dev'}, dimensions={0} | all-to-all | bytes 458752 | tf_op jit(solution)/shard_map/all_to_all | solution.py:111
  34.1 0.8 %reduce_sum.12 = bf16[2,7168]{1,0:T(2,128)(2,1)} reduce(bf16[8,2,7168]{2,1,0:T(2,128)(2,1)S(1)} %all_to_all.11, bf16[]{:T(256)} %constant.2.clone.1), dimensions={0}, to_apply=%region_0.0 | reduce | flops 100352 | bytes 258050 | tf_op jit(solution)/shard_map/reduce_sum | solution.py:112
  (1 shorter events, 0.0 us)
Async XLA Ops:
  0.9 17.4 %copy-start = (bf16[1,7168,256]{2,1,0:T(8,128)(2,1)S(1)}, bf16[1,7168,256]{2,1,0:T(8,128)(2,1)}, u32[]{:S(2)}) copy-start(bf16[1,7168,256]{2,1,0:T(8,128)(2,1)} %gate_ref.1) | copy-start | bytes 11010052
  0.9 17.4 %copy-start.1 = (bf16[1,7168,256]{2,1,0:T(8,128)(2,1)S(1)}, bf16[1,7168,256]{2,1,0:T(8,128)(2,1)}, u32[]{:S(2)}) copy-start(bf16[1,7168,256]{2,1,0:T(8,128)(2,1)} %up_ref.1) | copy-start | bytes 11010052
  0.9 17.4 %copy-start.2 = (bf16[1,256,7168]{2,1,0:T(8,128)(2,1)S(1)}, bf16[1,256,7168]{2,1,0:T(8,128)(2,1)}, u32[]{:S(2)}) copy-start(bf16[1,256,7168]{2,1,0:T(8,128)(2,1)} %down_ref.1) | copy-start | bytes 11010052
  16.8 1.5 %collective-permute-start = (bf16[8,2,7296]{2,1,0:T(2,128)(2,1)S(1)}, bf16[8,2,7296]{2,1,0:T(2,128)(2,1)S(1)}, u32[]{:S(2)}, u32[]{:S(2)}) collective-permute-start(bf16[8,2,7296]{2,1,0:T(2,128)(2,1)S(1)} %all_to_all.10.own_ref), channel_id=1, source_target_pairs={{0,8},{8,0},{1,9},{9,1},{2,10},{10,2},{3,11},{11,3},{4,12},{12,4},... | collective-permute-start | bytes 700424 | tf_op jit(solution)/shard_map/ppermute | solution.py:97
  20.4 1.6 %collective-permute-start.1 = (bf16[8,2,7168]{2,1,0:T(2,128)(2,1)S(1)}, bf16[8,2,7168]{2,1,0:T(2,128)(2,1)S(1)}, u32[]{:S(2)}, u32[]{:S(2)}) collective-permute-start(bf16[8,2,7168]{2,1,0:T(2,128)(2,1)S(1)} %get-tuple-element.16), channel_id=1, source_target_pairs={{0,8},{8,0},{1,9},{9,1},{2,10},{10,2},{3,11},{11,3},{4,12},{12,4},... | collective-permute-start | bytes 688136 | tf_op jit(solution)/shard_map/ppermute | solution.py:109

commit v6 on v5

--- a/solution.py
+++ b/solution.py
@@ -11,6 +11,7 @@
 SPARE = 2048
 SPACER_LIMIT = 38 * 1024 * 1024
 COLUMNS = 1024
+RING_OF_8 = (5, 4, 3, 2, 7, 6, 1, 0)
 
 
 def pack_kernel(tokens_ref, routes_ref, weights_ref, packed_ref, spare_ref):
@@ -73,6 +74,7 @@
     wide = width + -(-experts // LANES) * LANES
     vmem = pl.BlockSpec(memory_space=pltpu.VMEM)
     swap = [(i, i ^ 1) for i in range(nodes)]
+    order = [list(RING_OF_8 if devs == len(RING_OF_8) else range(devs))]
 
     packed, spare = pl.pallas_call(
         pack_kernel,
@@ -93,7 +95,9 @@
         name="spacer",
     )(packed, spare)
     packed, mark = lax.optimization_barrier((packed, mark))
-    own = lax.all_to_all(packed, "dev", split_axis=0, concat_axis=0, tiled=True)
+    own = lax.all_to_all(
+        packed, "dev", split_axis=0, concat_axis=0, tiled=True, axis_index_groups=order
+    )
     other = lax.ppermute(own, "node", swap)
     own_out, other_out = pl.pallas_call(
         expert_kernel,
@@ -108,7 +112,9 @@
     )(own, other, gate_weight, up_weight, down_weight, mark)
     arrived = lax.ppermute(other_out, "node", swap)
     partial = (own_out + arrived.astype(jnp.float32)).astype(jnp.bfloat16)
-    returned = lax.all_to_all(partial, "dev", split_axis=0, concat_axis=0, tiled=True)
+    returned = lax.all_to_all(
+        partial, "dev", split_axis=0, concat_axis=0, tiled=True, axis_index_groups=order
+    )
     return jnp.sum(returned.astype(jnp.float32), axis=0).astype(jnp.bfloat16)
 
 

time: 35.1 us -> 31.2 us (0.89)
  blocking collectives: 27.8 us -> 23.9 us
    all_to_all x2, blocking collectives: 27.8 us -> 23.9 us  [the longest x1 12.8 us: per_device(): lax.all_to_all(packed, 'dev', split_axis=0, concat_axis=0, tiled=True, ax...]
where the time goes in v6:
time: 31.2 us; the launch traced here: 31 us
  blocking collectives  23.9 us (77%)
  Pallas kernels  3 us (10%)
  waiting for transfers between devices  2.85 us (9%)
  other arithmetic  1.07 us (3%)
    all_to_all x1, blocking collectives, per_device(): lax.all_to_all(packed, 'dev', split_axis=0, concat_axis=0, tiled=True, ax...  12.8 us
    all_to_all x1, blocking collectives, per_device(): lax.all_to_all(partial, 'dev', split_axis=0, concat_axis=0, tiled=True, a...  11 us
    pallas_call x1, Pallas kernels, per_device(): pl.pallas_call(expert_kernel, out_shape=(jax.ShapeDtypeStruct((devs, tok_...  2.09 us
    ppermute x1, waiting for transfers between devices, per_device(): other = lax.ppermute(own, 'node', swap)  1.49 us
    ppermute x1, waiting for transfers between devices, per_device(): arrived = lax.ppermute(other_out, 'node', swap)  1.35 us
    pallas_call x1, Pallas kernels, per_device(): pl.pallas_call(pack_kernel, out_shape=(pltpu.VMEM((devs, tok_rows, wide),...  0.91 us
    reduce_sum x1, other arithmetic, per_device(): return jnp.sum(returned.astype(jnp.float32), axis=0).astype(jnp.bfloat16)  0.82 us
  transfers between devices with their start and end apart: 2, of which 2 were waited for; matrix products, arithmetic and copies ran while one was open for 0% of the time, Pallas kernels for 0%

profile of v6, /device:TPU:0, one launch (start us, length us, event | category | flops | bytes accessed | tf_op | source)
XLA Modules:
  0.0 31.0 jit_solution(16151541332179554380)
XLA Ops:
  0.0 0.9 %pack.1 = (bf16[8,2,7296]{2,1,0:T(2,128)(2,1)S(1)}, bf16[2048,7168]{1,0:T(8,128)(2,1)}) custom-call(bf16[2,7168]{1,0:T(2,128)(2,1)} %tokens_ref.1, s32[1,2]{1,0:T(1,128)} %bitcast.1, bf16[2,1]{1,0:T(2,128)(2,1)} %weights_ref.1), custom_call_target="tpu_custom_call" | custom-call | tf_op jit(solution)/shard_map/pack/pallas_call | solution.py:79
  0.9 0.0 copy-start
  0.9 0.0 copy-start.1
  0.9 0.0 copy-start.2
  0.9 12.8 %all_to_all.10.own_ref = bf16[8,2,7296]{2,1,0:T(2,128)(2,1)S(1)} all-to-all(bf16[8,2,7296]{2,1,0:T(2,128)(2,1)S(1)} %get-tuple-element.13.packed_ref), channel_id=1, replica_groups={{5,4,3,2,7,6,1,0},{13,12,11,10,15,14,9,8},{21,20,19,18,23,22,17,16},{29..., dimensions={0} | all-to-all | bytes 466944 | tf_op jit(solution)/shard_map/all_to_all | solution.py:98
  13.8 0.0 collective-permute-start
  13.8 1.5 %collective-permute-done.other_ref = bf16[8,2,7296]{2,1,0:T(2,128)(2,1)S(1)} collective-permute-done((bf16[8,2,7296]{2,1,0:T(2,128)(2,1)S(1)}, bf16[8,2,7296]{2,1,0:T(2,128)(2,1)S(1)}, u32[]{:S(2)}, u32[]{:S(2)}) %collective-permute-start) | collective-permute-done | bytes 233504 | tf_op jit(solution)/shard_map/ppermute | solution.py:101
  15.3 0.0 copy-done
  15.3 0.0 copy-done.1
  15.3 0.0 copy-done.2
  15.3 2.1 %expert.1 = (f32[8,2,7168]{2,1,0:T(2,128)S(1)}, bf16[8,2,7168]{2,1,0:T(2,128)(2,1)S(1)}) custom-call(bf16[8,2,7296]{2,1,0:T(2,128)(2,1)S(1)} %all_to_all.10.own_ref, bf16[8,2,7296]{2,1,0:T(2,128)(2,1)S(1)} %collective-permute-done.other_ref, bf16[1,7168,256]{2,1,0:T(8,128)(2,1)S(1)} %copy-done, bf16[1,7168,256]{2,1,0:T(8,128)(2,1)S(1)} %copy-done.1, ...), custom_call_target="tpu_custom_call" | custom-call | tf_op jit(solution)/shard_map/expert/pallas_call | solution.py:102
  17.4 0.2 collective-permute-start.1
  17.6 1.4 %collective-permute-done.1 = bf16[8,2,7168]{2,1,0:T(2,128)(2,1)S(1)} collective-permute-done((bf16[8,2,7168]{2,1,0:T(2,128)(2,1)S(1)}, bf16[8,2,7168]{2,1,0:T(2,128)(2,1)S(1)}, u32[]{:S(2)}, u32[]{:S(2)}) %collective-permute-start.1) | collective-permute-done | bytes 229408 | tf_op jit(solution)/shard_map/ppermute | solution.py:113
  18.9 0.3 add_convert_fusion
  19.2 11.0 %all_to_all.11 = bf16[8,2,7168]{2,1,0:T(2,128)(2,1)S(1)} all-to-all(bf16[8,2,7168]{2,1,0:T(2,128)(2,1)S(1)} %add_convert_fusion), channel_id=1, replica_groups={{5,4,3,2,7,6,1,0},{13,12,11,10,15,14,9,8},{21,20,19,18,23,22,17,16},{29..., dimensions={0} | all-to-all | bytes 458752 | tf_op jit(solution)/shard_map/all_to_all | solution.py:115
  30.2 0.8 %reduce_sum.12 = bf16[2,7168]{1,0:T(2,128)(2,1)} reduce(bf16[8,2,7168]{2,1,0:T(2,128)(2,1)S(1)} %all_to_all.11, bf16[]{:T(256)} %constant.2.clone.1), dimensions={0}, to_apply=%region_0.0 | reduce | flops 100352 | bytes 258050 | tf_op jit(solution)/shard_map/reduce_sum | solution.py:118
  (1 shorter events, 0.0 us)
Async XLA Ops:
  0.9 14.3 %copy-start = (bf16[1,7168,256]{2,1,0:T(8,128)(2,1)S(1)}, bf16[1,7168,256]{2,1,0:T(8,128)(2,1)}, u32[]{:S(2)}) copy-start(bf16[1,7168,256]{2,1,0:T(8,128)(2,1)} %gate_ref.1) | copy-start | bytes 11010052
  0.9 14.3 %copy-start.1 = (bf16[1,7168,256]{2,1,0:T(8,128)(2,1)S(1)}, bf16[1,7168,256]{2,1,0:T(8,128)(2,1)}, u32[]{:S(2)}) copy-start(bf16[1,7168,256]{2,1,0:T(8,128)(2,1)} %up_ref.1) | copy-start | bytes 11010052
  0.9 14.4 %copy-start.2 = (bf16[1,256,7168]{2,1,0:T(8,128)(2,1)S(1)}, bf16[1,256,7168]{2,1,0:T(8,128)(2,1)}, u32[]{:S(2)}) copy-start(bf16[1,256,7168]{2,1,0:T(8,128)(2,1)} %down_ref.1) | copy-start | bytes 11010052
  13.8 1.5 %collective-permute-start = (bf16[8,2,7296]{2,1,0:T(2,128)(2,1)S(1)}, bf16[8,2,7296]{2,1,0:T(2,128)(2,1)S(1)}, u32[]{:S(2)}, u32[]{:S(2)}) collective-permute-start(bf16[8,2,7296]{2,1,0:T(2,128)(2,1)S(1)} %all_to_all.10.own_ref), channel_id=1, source_target_pairs={{0,8},{8,0},{1,9},{9,1},{2,10},{10,2},{3,11},{11,3},{4,12},{12,4},... | collective-permute-start | bytes 700424 | tf_op jit(solution)/shard_map/ppermute | solution.py:101
  17.4 1.6 %collective-permute-start.1 = (bf16[8,2,7168]{2,1,0:T(2,128)(2,1)S(1)}, bf16[8,2,7168]{2,1,0:T(2,128)(2,1)S(1)}, u32[]{:S(2)}, u32[]{:S(2)}) collective-permute-start(bf16[8,2,7168]{2,1,0:T(2,128)(2,1)S(1)} %get-tuple-element.16), channel_id=1, source_target_pairs={{0,8},{8,0},{1,9},{9,1},{2,10},{10,2},{3,11},{11,3},{4,12},{12,4},... | collective-permute-start | bytes 688136 | tf_op jit(solution)/shard_map/ppermute | solution.py:113

commit v7 on v6

--- a/solution.py
+++ b/solution.py
@@ -11,7 +11,8 @@
 SPARE = 2048
 SPACER_LIMIT = 38 * 1024 * 1024
 COLUMNS = 1024
-RING_OF_8 = (5, 4, 3, 2, 7, 6, 1, 0)
+SEND_ORDERS = ((5, 3, 4, 0, 7, 1, 2, 6), (5, 7, 4, 0, 1, 3, 2, 6))
+RETURN_ORDERS = ((5, 4, 3, 2, 7, 6, 1, 0), (4, 0, 2, 7, 1, 6, 5, 3))
 
 
 def pack_kernel(tokens_ref, routes_ref, weights_ref, packed_ref, spare_ref):
@@ -34,6 +35,23 @@
     mark_ref[...] = jnp.zeros_like(mark_ref)
 
 
+def reorder_matrix(devs, tok_rows):
+    half = devs * tok_rows
+    shape = (2 * half, 2 * half)
+    place = lax.broadcasted_iota(jnp.int32, shape, 0)
+    source = lax.broadcasted_iota(jnp.int32, shape, 1)
+    node = lax.axis_index("node")
+    core = jnp.where(place < half, node, 1 - node)
+    wanted = jnp.zeros(shape, jnp.int32)
+    for c in range(2):
+        for q in range(devs):
+            held = SEND_ORDERS[c].index(RETURN_ORDERS[c][q])
+            here = (core == c) & (place % half // tok_rows == q)
+            wanted = jnp.where(here, held * tok_rows, wanted)
+    wanted += place // half * half + place % tok_rows
+    return (source == wanted).astype(jnp.bfloat16)
+
+
 def expert_kernel(own_ref, other_ref, gate_ref, up_ref, down_ref, mark_ref, own_out, other_out):
     devs, tok_rows, wide = own_ref.shape
     _, width, hidden_units = gate_ref.shape
@@ -44,7 +62,11 @@
         return jnp.concatenate([half.reshape(rows, half.shape[2]) for half in halves], axis=0)
 
     expert = lax.axis_index("node") * (lax.axis_size("dev") // SPLIT) + lax.axis_index("dev") // SPLIT
-    combine = tokens_part(slice(width, wide)).astype(jnp.float32)
+    combine = tokens_part(slice(width, wide))
+    if devs == len(SEND_ORDERS[0]):
+        reorder = reorder_matrix(devs, tok_rows)
+        combine = jnp.dot(reorder, combine, preferred_element_type=jnp.float32)
+    combine = combine.astype(jnp.float32)
     columns = lax.broadcasted_iota(jnp.int32, combine.shape, 1)
     scale = jnp.sum(jnp.where(columns == expert, combine, 0.0), axis=1, keepdims=True)
     gate = jnp.zeros((2 * rows, hidden_units), jnp.float32)
@@ -55,6 +77,8 @@
         gate += jnp.dot(block, gate_ref[0, part, :], preferred_element_type=jnp.float32)
         upper += jnp.dot(block, up_ref[0, part, :], preferred_element_type=jnp.float32)
     hidden = (gate / (1.0 + jnp.exp(-gate)) * upper).astype(jnp.bfloat16)
+    if devs == len(SEND_ORDERS[0]):
+        hidden = jnp.dot(reorder, hidden, preferred_element_type=jnp.float32).astype(jnp.bfloat16)
     for start in range(0, width, COLUMNS):
         part = slice(start, start + COLUMNS)
         output = scale * jnp.dot(
@@ -74,7 +98,13 @@
     wide = width + -(-experts // LANES) * LANES
     vmem = pl.BlockSpec(memory_space=pltpu.VMEM)
     swap = [(i, i ^ 1) for i in range(nodes)]
-    order = [list(RING_OF_8 if devs == len(RING_OF_8) else range(devs))]
+    if devs == len(SEND_ORDERS[0]):
+        orders = (SEND_ORDERS, RETURN_ORDERS)
+    else:
+        orders = ((tuple(range(devs)),) * nodes,) * 2
+    send_groups, return_groups = (
+        [[node * devs + dev for dev in order[node]] for node in range(nodes)] for order in orders
+    )
 
     packed, spare = pl.pallas_call(
         pack_kernel,
@@ -96,7 +126,8 @@
     )(packed, spare)
     packed, mark = lax.optimization_barrier((packed, mark))
     own = lax.all_to_all(
-        packed, "dev", split_axis=0, concat_axis=0, tiled=True, axis_index_groups=order
+        packed, ("node", "dev"), split_axis=0, concat_axis=0, tiled=True,
+        axis_index_groups=send_groups,
     )
     other = lax.ppermute(own, "node", swap)
     own_out, other_out = pl.pallas_call(
@@ -113,7 +144,8 @@
     arrived = lax.ppermute(other_out, "node", swap)
     partial = (own_out + arrived.astype(jnp.float32)).astype(jnp.bfloat16)
     returned = lax.all_to_all(
-        partial, "dev", split_axis=0, concat_axis=0, tiled=True, axis_index_groups=order
+        partial, ("node", "dev"), split_axis=0, concat_axis=0, tiled=True,
+        axis_index_groups=return_groups,
     )
     return jnp.sum(returned.astype(jnp.float32), axis=0).astype(jnp.bfloat16)
 

time: 31.2 us -> 30.6 us (0.981)
  blocking collectives: 23.9 us -> 23.2 us
    all_to_all x2, blocking collectives: 23.9 us -> 23.2 us  [the longest x1 13.8 us: per_device(): lax.all_to_all(packed, ('node', 'dev'), split_axis=0, concat_axis=0, tile...]
where the time goes in v7:
time: 30.6 us; the launch traced here: 30.4 us
  blocking collectives  23.2 us (76%)
  Pallas kernels  3.04 us (10%)
  waiting for transfers between devices  2.84 us (9%)
  other arithmetic  1.07 us (3%)
    all_to_all x1, blocking collectives, per_device(): lax.all_to_all(packed, ('node', 'dev'), split_axis=0, concat_axis=0, tile...  13.8 us
    all_to_all x1, blocking collectives, per_device(): lax.all_to_all(partial, ('node', 'dev'), split_axis=0, concat_axis=0, til...  9.41 us
    pallas_call x1, Pallas kernels, per_device(): pl.pallas_call(expert_kernel, out_shape=(jax.ShapeDtypeStruct((devs, tok_...  2.13 us
    ppermute x1, waiting for transfers between devices, per_device(): other = lax.ppermute(own, 'node', swap)  1.49 us
    ppermute x1, waiting for transfers between devices, per_device(): arrived = lax.ppermute(other_out, 'node', swap)  1.35 us
    pallas_call x1, Pallas kernels, per_device(): pl.pallas_call(pack_kernel, out_shape=(pltpu.VMEM((devs, tok_rows, wide),...  0.91 us
    reduce_sum x1, other arithmetic, per_device(): return jnp.sum(returned.astype(jnp.float32), axis=0).astype(jnp.bfloat16)  0.82 us
  transfers between devices with their start and end apart: 2, of which 2 were waited for; matrix products, arithmetic and copies ran while one was open for 0% of the time, Pallas kernels for 0%

profile of v7, /device:TPU:0, one launch (start us, length us, event | category | flops | bytes accessed | tf_op | source)
XLA Modules:
  0.0 30.4 jit_solution(662058846037306538)
XLA Ops:
  0.0 0.9 %pack.1 = (bf16[8,2,7296]{2,1,0:T(2,128)(2,1)S(1)}, bf16[2048,7168]{1,0:T(8,128)(2,1)}) custom-call(bf16[2,7168]{1,0:T(2,128)(2,1)} %tokens_ref.1, s32[1,2]{1,0:T(1,128)} %bitcast.1, bf16[2,1]{1,0:T(2,128)(2,1)} %weights_ref.1), custom_call_target="tpu_custom_call" | custom-call | tf_op jit(solution)/shard_map/pack/pallas_call | solution.py:109
  0.9 0.0 copy-start
  0.9 0.0 copy-start.1
  0.9 0.0 copy-start.2
  0.9 13.8 %all_to_all.10.own_ref = bf16[8,2,7296]{2,1,0:T(2,128)(2,1)S(1)} all-to-all(bf16[8,2,7296]{2,1,0:T(2,128)(2,1)S(1)} %get-tuple-element.13.packed_ref), channel_id=1, replica_groups={{5,3,4,0,7,1,2,6},{13,15,12,8,9,11,10,14},{21,19,20,16,23,17,18,22},{29..., dimensions={0} | all-to-all | bytes 466944 | tf_op jit(solution)/shard_map/all_to_all | solution.py:128
  14.7 0.0 collective-permute-start
  14.7 1.5 %collective-permute-done.other_ref = bf16[8,2,7296]{2,1,0:T(2,128)(2,1)S(1)} collective-permute-done((bf16[8,2,7296]{2,1,0:T(2,128)(2,1)S(1)}, bf16[8,2,7296]{2,1,0:T(2,128)(2,1)S(1)}, u32[]{:S(2)}, u32[]{:S(2)}) %collective-permute-start) | collective-permute-done | bytes 233504 | tf_op jit(solution)/shard_map/ppermute | solution.py:132
  16.2 0.0 copy-done
  16.2 0.0 copy-done.1
  16.2 0.0 copy-done.2
  16.2 2.1 %expert.1 = (f32[8,2,7168]{2,1,0:T(2,128)S(1)}, bf16[8,2,7168]{2,1,0:T(2,128)(2,1)S(1)}) custom-call(bf16[8,2,7296]{2,1,0:T(2,128)(2,1)S(1)} %all_to_all.10.own_ref, bf16[8,2,7296]{2,1,0:T(2,128)(2,1)S(1)} %collective-permute-done.other_ref, bf16[1,7168,256]{2,1,0:T(8,128)(2,1)S(1)} %copy-done, bf16[1,7168,256]{2,1,0:T(8,128)(2,1)S(1)} %copy-done.1, ...), custom_call_target="tpu_custom_call" | custom-call | tf_op jit(solution)/shard_map/expert/pallas_call | solution.py:133
  18.3 0.2 collective-permute-start.1
  18.6 1.4 %collective-permute-done.1 = bf16[8,2,7168]{2,1,0:T(2,128)(2,1)S(1)} collective-permute-done((bf16[8,2,7168]{2,1,0:T(2,128)(2,1)S(1)}, bf16[8,2,7168]{2,1,0:T(2,128)(2,1)S(1)}, u32[]{:S(2)}, u32[]{:S(2)}) %collective-permute-start.1) | collective-permute-done | bytes 229408 | tf_op jit(solution)/shard_map/ppermute | solution.py:144
  19.9 0.3 add_convert_fusion
  20.2 9.4 %all_to_all.11 = bf16[8,2,7168]{2,1,0:T(2,128)(2,1)S(1)} all-to-all(bf16[8,2,7168]{2,1,0:T(2,128)(2,1)S(1)} %add_convert_fusion), channel_id=1, replica_groups={{5,4,3,2,7,6,1,0},{12,8,10,15,9,14,13,11},{21,20,19,18,23,22,17,16},{28..., dimensions={0} | all-to-all | bytes 458752 | tf_op jit(solution)/shard_map/all_to_all | solution.py:146
  29.6 0.8 %reduce_sum.12 = bf16[2,7168]{1,0:T(2,128)(2,1)} reduce(bf16[8,2,7168]{2,1,0:T(2,128)(2,1)S(1)} %all_to_all.11, bf16[]{:T(256)} %constant.2.clone.1), dimensions={0}, to_apply=%region_0.0 | reduce | flops 100352 | bytes 258050 | tf_op jit(solution)/shard_map/reduce_sum | solution.py:150
  (1 shorter events, 0.0 us)
Async XLA Ops:
  0.9 15.3 %copy-start = (bf16[1,7168,256]{2,1,0:T(8,128)(2,1)S(1)}, bf16[1,7168,256]{2,1,0:T(8,128)(2,1)}, u32[]{:S(2)}) copy-start(bf16[1,7168,256]{2,1,0:T(8,128)(2,1)} %gate_ref.1) | copy-start | bytes 11010052
  0.9 15.3 %copy-start.1 = (bf16[1,7168,256]{2,1,0:T(8,128)(2,1)S(1)}, bf16[1,7168,256]{2,1,0:T(8,128)(2,1)}, u32[]{:S(2)}) copy-start(bf16[1,7168,256]{2,1,0:T(8,128)(2,1)} %up_ref.1) | copy-start | bytes 11010052
  0.9 15.3 %copy-start.2 = (bf16[1,256,7168]{2,1,0:T(8,128)(2,1)S(1)}, bf16[1,256,7168]{2,1,0:T(8,128)(2,1)}, u32[]{:S(2)}) copy-start(bf16[1,256,7168]{2,1,0:T(8,128)(2,1)} %down_ref.1) | copy-start | bytes 11010052
  14.7 1.5 %collective-permute-start = (bf16[8,2,7296]{2,1,0:T(2,128)(2,1)S(1)}, bf16[8,2,7296]{2,1,0:T(2,128)(2,1)S(1)}, u32[]{:S(2)}, u32[]{:S(2)}) collective-permute-start(bf16[8,2,7296]{2,1,0:T(2,128)(2,1)S(1)} %all_to_all.10.own_ref), channel_id=1, source_target_pairs={{0,8},{8,0},{1,9},{9,1},{2,10},{10,2},{3,11},{11,3},{4,12},{12,4},... | collective-permute-start | bytes 700424 | tf_op jit(solution)/shard_map/ppermute | solution.py:132
  18.3 1.6 %collective-permute-start.1 = (bf16[8,2,7168]{2,1,0:T(2,128)(2,1)S(1)}, bf16[8,2,7168]{2,1,0:T(2,128)(2,1)S(1)}, u32[]{:S(2)}, u32[]{:S(2)}) collective-permute-start(bf16[8,2,7168]{2,1,0:T(2,128)(2,1)S(1)} %get-tuple-element.16), channel_id=1, source_target_pairs={{0,8},{8,0},{1,9},{9,1},{2,10},{10,2},{3,11},{11,3},{4,12},{12,4},... | collective-permute-start | bytes 688136 | tf_op jit(solution)/shard_map/ppermute | solution.py:144

commit v8 on v7

--- a/solution.py
+++ b/solution.py
@@ -11,8 +11,8 @@
 SPARE = 2048
 SPACER_LIMIT = 38 * 1024 * 1024
 COLUMNS = 1024
-SEND_ORDERS = ((5, 3, 4, 0, 7, 1, 2, 6), (5, 7, 4, 0, 1, 3, 2, 6))
-RETURN_ORDERS = ((5, 4, 3, 2, 7, 6, 1, 0), (4, 0, 2, 7, 1, 6, 5, 3))
+SEND_ORDERS = ((5, 7, 4, 0, 3, 1, 2, 6), (5, 0, 3, 2, 4, 1, 7, 6))
+RETURN_ORDERS = ((5, 4, 3, 0, 7, 6, 1, 2), (4, 0, 2, 7, 1, 6, 5, 3))
 
 
 def pack_kernel(tokens_ref, routes_ref, weights_ref, packed_ref, spare_ref):

time: 30.6 us -> 30.2 us (0.987)
  blocking collectives: 23.2 us -> 22.8 us
    all_to_all x1, blocking collectives: 9.41 us -> 9 us  [per_device(): lax.all_to_all(partial, ('node', 'dev'), split_axis=0, concat_axis=0, til...]
where the time goes in v8:
time: 30.2 us; the launch traced here: 30 us
  blocking collectives  22.8 us (75%)
  Pallas kernels  3.04 us (10%)
  waiting for transfers between devices  2.85 us (9%)
  other arithmetic  1.07 us (4%)
    all_to_all x1, blocking collectives, per_device(): lax.all_to_all(packed, ('node', 'dev'), split_axis=0, concat_axis=0, tile...  13.8 us
    all_to_all x1, blocking collectives, per_device(): lax.all_to_all(partial, ('node', 'dev'), split_axis=0, concat_axis=0, til...  9 us
    pallas_call x1, Pallas kernels, per_device(): pl.pallas_call(expert_kernel, out_shape=(jax.ShapeDtypeStruct((devs, tok_...  2.13 us
    ppermute x1, waiting for transfers between devices, per_device(): other = lax.ppermute(own, 'node', swap)  1.49 us
    ppermute x1, waiting for transfers between devices, per_device(): arrived = lax.ppermute(other_out, 'node', swap)  1.36 us
    pallas_call x1, Pallas kernels, per_device(): pl.pallas_call(pack_kernel, out_shape=(pltpu.VMEM((devs, tok_rows, wide),...  0.91 us
    reduce_sum x1, other arithmetic, per_device(): return jnp.sum(returned.astype(jnp.float32), axis=0).astype(jnp.bfloat16)  0.82 us
  transfers between devices with their start and end apart: 2, of which 2 were waited for; matrix products, arithmetic and copies ran while one was open for 0% of the time, Pallas kernels for 0%

profile of v8, /device:TPU:0, one launch (start us, length us, event | category | flops | bytes accessed | tf_op | source)
XLA Modules:
  0.0 30.0 jit_solution(244710069326646466)
XLA Ops:
  0.0 0.9 %pack.1 = (bf16[8,2,7296]{2,1,0:T(2,128)(2,1)S(1)}, bf16[2048,7168]{1,0:T(8,128)(2,1)}) custom-call(bf16[2,7168]{1,0:T(2,128)(2,1)} %tokens_ref.1, s32[1,2]{1,0:T(1,128)} %bitcast.1, bf16[2,1]{1,0:T(2,128)(2,1)} %weights_ref.1), custom_call_target="tpu_custom_call" | custom-call | tf_op jit(solution)/shard_map/pack/pallas_call | solution.py:109
  0.9 0.0 copy-start
  0.9 0.0 copy-start.1
  0.9 0.0 copy-start.2
  0.9 13.8 %all_to_all.10.own_ref = bf16[8,2,7296]{2,1,0:T(2,128)(2,1)S(1)} all-to-all(bf16[8,2,7296]{2,1,0:T(2,128)(2,1)S(1)} %get-tuple-element.13.packed_ref), channel_id=1, replica_groups={{5,7,4,0,3,1,2,6},{13,8,11,10,12,9,15,14},{21,23,20,16,19,17,18,22},{29..., dimensions={0} | all-to-all | bytes 466944 | tf_op jit(solution)/shard_map/all_to_all | solution.py:128
  14.7 0.0 collective-permute-start
  14.7 1.5 %collective-permute-done.other_ref = bf16[8,2,7296]{2,1,0:T(2,128)(2,1)S(1)} collective-permute-done((bf16[8,2,7296]{2,1,0:T(2,128)(2,1)S(1)}, bf16[8,2,7296]{2,1,0:T(2,128)(2,1)S(1)}, u32[]{:S(2)}, u32[]{:S(2)}) %collective-permute-start) | collective-permute-done | bytes 233504 | tf_op jit(solution)/shard_map/ppermute | solution.py:132
  16.2 0.0 copy-done
  16.2 0.0 copy-done.1
  16.2 0.0 copy-done.2
  16.2 2.1 %expert.1 = (f32[8,2,7168]{2,1,0:T(2,128)S(1)}, bf16[8,2,7168]{2,1,0:T(2,128)(2,1)S(1)}) custom-call(bf16[8,2,7296]{2,1,0:T(2,128)(2,1)S(1)} %all_to_all.10.own_ref, bf16[8,2,7296]{2,1,0:T(2,128)(2,1)S(1)} %collective-permute-done.other_ref, bf16[1,7168,256]{2,1,0:T(8,128)(2,1)S(1)} %copy-done, bf16[1,7168,256]{2,1,0:T(8,128)(2,1)S(1)} %copy-done.1, ...), custom_call_target="tpu_custom_call" | custom-call | tf_op jit(solution)/shard_map/expert/pallas_call | solution.py:133
  18.4 0.2 collective-permute-start.1
  18.6 1.4 %collective-permute-done.1 = bf16[8,2,7168]{2,1,0:T(2,128)(2,1)S(1)} collective-permute-done((bf16[8,2,7168]{2,1,0:T(2,128)(2,1)S(1)}, bf16[8,2,7168]{2,1,0:T(2,128)(2,1)S(1)}, u32[]{:S(2)}, u32[]{:S(2)}) %collective-permute-start.1) | collective-permute-done | bytes 229408 | tf_op jit(solution)/shard_map/ppermute | solution.py:144
  19.9 0.3 add_convert_fusion
  20.2 9.0 %all_to_all.11 = bf16[8,2,7168]{2,1,0:T(2,128)(2,1)S(1)} all-to-all(bf16[8,2,7168]{2,1,0:T(2,128)(2,1)S(1)} %add_convert_fusion), channel_id=1, replica_groups={{5,4,3,0,7,6,1,2},{12,8,10,15,9,14,13,11},{21,20,19,16,23,22,17,18},{28..., dimensions={0} | all-to-all | bytes 458752 | tf_op jit(solution)/shard_map/all_to_all | solution.py:146
  29.2 0.8 %reduce_sum.12 = bf16[2,7168]{1,0:T(2,128)(2,1)} reduce(bf16[8,2,7168]{2,1,0:T(2,128)(2,1)S(1)} %all_to_all.11, bf16[]{:T(256)} %constant.2.clone.1), dimensions={0}, to_apply=%region_0.0 | reduce | flops 100352 | bytes 258050 | tf_op jit(solution)/shard_map/reduce_sum | solution.py:150
  (1 shorter events, 0.0 us)
Async XLA Ops:
  0.9 15.3 %copy-start = (bf16[1,7168,256]{2,1,0:T(8,128)(2,1)S(1)}, bf16[1,7168,256]{2,1,0:T(8,128)(2,1)}, u32[]{:S(2)}) copy-start(bf16[1,7168,256]{2,1,0:T(8,128)(2,1)} %gate_ref.1) | copy-start | bytes 11010052
  0.9 15.3 %copy-start.1 = (bf16[1,7168,256]{2,1,0:T(8,128)(2,1)S(1)}, bf16[1,7168,256]{2,1,0:T(8,128)(2,1)}, u32[]{:S(2)}) copy-start(bf16[1,7168,256]{2,1,0:T(8,128)(2,1)} %up_ref.1) | copy-start | bytes 11010052
  0.9 15.3 %copy-start.2 = (bf16[1,256,7168]{2,1,0:T(8,128)(2,1)S(1)}, bf16[1,256,7168]{2,1,0:T(8,128)(2,1)}, u32[]{:S(2)}) copy-start(bf16[1,256,7168]{2,1,0:T(8,128)(2,1)} %down_ref.1) | copy-start | bytes 11010052
  14.7 1.5 %collective-permute-start = (bf16[8,2,7296]{2,1,0:T(2,128)(2,1)S(1)}, bf16[8,2,7296]{2,1,0:T(2,128)(2,1)S(1)}, u32[]{:S(2)}, u32[]{:S(2)}) collective-permute-start(bf16[8,2,7296]{2,1,0:T(2,128)(2,1)S(1)} %all_to_all.10.own_ref), channel_id=1, source_target_pairs={{0,8},{8,0},{1,9},{9,1},{2,10},{10,2},{3,11},{11,3},{4,12},{12,4},... | collective-permute-start | bytes 700424 | tf_op jit(solution)/shard_map/ppermute | solution.py:132
  18.4 1.6 %collective-permute-start.1 = (bf16[8,2,7168]{2,1,0:T(2,128)(2,1)S(1)}, bf16[8,2,7168]{2,1,0:T(2,128)(2,1)S(1)}, u32[]{:S(2)}, u32[]{:S(2)}) collective-permute-start(bf16[8,2,7168]{2,1,0:T(2,128)(2,1)S(1)} %get-tuple-element.16), channel_id=1, source_target_pairs={{0,8},{8,0},{1,9},{9,1},{2,10},{10,2},{3,11},{11,3},{4,12},{12,4},... | collective-permute-start | bytes 688136 | tf_op jit(solution)/shard_map/ppermute | solution.py:144

commit v9 on v8

--- a/solution.py
+++ b/solution.py
@@ -84,9 +84,8 @@
         output = scale * jnp.dot(
             hidden, down_ref[0, :, part], preferred_element_type=jnp.float32
         )
-        own_out[:, :, part] = output[:rows].reshape(devs, tok_rows, COLUMNS)
-        other = output[rows:].astype(jnp.bfloat16)
-        other_out[:, :, part] = other.reshape(devs, tok_rows, COLUMNS)
+        own_out[:, part] = output[:rows]
+        other_out[:, part] = output[rows:].astype(jnp.bfloat16)
 
 
 def per_device(tokens, routes, route_weights, gate_weight, up_weight, down_weight):
@@ -133,8 +132,8 @@
     own_out, other_out = pl.pallas_call(
         expert_kernel,
         out_shape=(
-            jax.ShapeDtypeStruct((devs, tok_rows, width), jnp.float32),
-            jax.ShapeDtypeStruct((devs, tok_rows, width), jnp.bfloat16),
+            jax.ShapeDtypeStruct((devs * tok_rows, width), jnp.float32),
+            jax.ShapeDtypeStruct((devs * tok_rows, width), jnp.bfloat16),
         ),
         in_specs=[vmem] * 6,
         out_specs=(vmem, vmem),
@@ -143,6 +142,7 @@
     )(own, other, gate_weight, up_weight, down_weight, mark)
     arrived = lax.ppermute(other_out, "node", swap)
     partial = (own_out + arrived.astype(jnp.float32)).astype(jnp.bfloat16)
+    partial = partial.reshape(devs, tok_rows, width)
     returned = lax.all_to_all(
         partial, ("node", "dev"), split_axis=0, concat_axis=0, tiled=True,
         axis_index_groups=return_groups,

time: 30.2 us -> 30.1 us (level)
  no operation moved by 1% of the time
where the time goes in v9:
time: 30.1 us; the launch traced here: 29.8 us
  blocking collectives  22.8 us (76%)
  Pallas kernels  3.03 us (10%)
  waiting for transfers between devices  2.85 us (9%)
  other arithmetic  0.87 us (3%)
    all_to_all x1, blocking collectives, per_device(): lax.all_to_all(packed, ('node', 'dev'), split_axis=0, concat_axis=0, tile...  13.8 us
    all_to_all x1, blocking collectives, per_device(): lax.all_to_all(partial, ('node', 'dev'), split_axis=0, concat_axis=0, til...  9 us
    pallas_call x1, Pallas kernels, per_device(): pl.pallas_call(expert_kernel, out_shape=(jax.ShapeDtypeStruct((devs * tok...  2.12 us
    ppermute x1, waiting for transfers between devices, per_device(): other = lax.ppermute(own, 'node', swap)  1.49 us
    ppermute x1, waiting for transfers between devices, per_device(): arrived = lax.ppermute(other_out, 'node', swap)  1.35 us
    pallas_call x1, Pallas kernels, per_device(): pl.pallas_call(pack_kernel, out_shape=(pltpu.VMEM((devs, tok_rows, wide),...  0.91 us
    reduce_sum x1, other arithmetic, per_device(): return jnp.sum(returned.astype(jnp.float32), axis=0).astype(jnp.bfloat16)  0.82 us
  transfers between devices with their start and end apart: 2, of which 2 were waited for; matrix products, arithmetic and copies ran while one was open for 0% of the time, Pallas kernels for 0%

profile of v9, /device:TPU:0, one launch (start us, length us, event | category | flops | bytes accessed | tf_op | source)
XLA Modules:
  0.0 29.8 jit_solution(5081948309460412884)
XLA Ops:
  0.0 0.9 %pack.1 = (bf16[8,2,7296]{2,1,0:T(2,128)(2,1)S(1)}, bf16[2048,7168]{1,0:T(8,128)(2,1)}) custom-call(bf16[2,7168]{1,0:T(2,128)(2,1)} %tokens_ref.1, s32[1,2]{1,0:T(1,128)} %bitcast.1, bf16[2,1]{1,0:T(2,128)(2,1)} %weights_ref.1), custom_call_target="tpu_custom_call" | custom-call | tf_op jit(solution)/shard_map/pack/pallas_call | solution.py:108
  0.9 0.0 copy-start
  0.9 0.0 copy-start.1
  0.9 0.0 copy-start.2
  0.9 13.8 %all_to_all.10.own_ref = bf16[8,2,7296]{2,1,0:T(2,128)(2,1)S(1)} all-to-all(bf16[8,2,7296]{2,1,0:T(2,128)(2,1)S(1)} %get-tuple-element.13.packed_ref), channel_id=1, replica_groups={{5,7,4,0,3,1,2,6},{13,8,11,10,12,9,15,14},{21,23,20,16,19,17,18,22},{29..., dimensions={0} | all-to-all | bytes 466944 | tf_op jit(solution)/shard_map/all_to_all | solution.py:127
  14.7 0.0 collective-permute-start
  14.7 1.5 %collective-permute-done.other_ref = bf16[8,2,7296]{2,1,0:T(2,128)(2,1)S(1)} collective-permute-done((bf16[8,2,7296]{2,1,0:T(2,128)(2,1)S(1)}, bf16[8,2,7296]{2,1,0:T(2,128)(2,1)S(1)}, u32[]{:S(2)}, u32[]{:S(2)}) %collective-permute-start) | collective-permute-done | bytes 233504 | tf_op jit(solution)/shard_map/ppermute | solution.py:131
  16.2 0.0 copy-done
  16.2 0.0 copy-done.1
  16.2 0.0 copy-done.2
  16.2 2.1 %expert.1 = (f32[16,7168]{1,0:T(8,128)S(1)}, bf16[16,7168]{1,0:T(8,128)(2,1)S(1)}) custom-call(bf16[8,2,7296]{2,1,0:T(2,128)(2,1)S(1)} %all_to_all.10.own_ref, bf16[8,2,7296]{2,1,0:T(2,128)(2,1)S(1)} %collective-permute-done.other_ref, bf16[1,7168,256]{2,1,0:T(8,128)(2,1)S(1)} %copy-done, bf16[1,7168,256]{2,1,0:T(8,128)(2,1)S(1)} %copy-done.1, ...), custom_call_target="tpu_custom_call" | custom-call | tf_op jit(solution)/shard_map/expert/pallas_call | solution.py:132
  18.3 0.2 collective-permute-start.1
  18.5 1.4 %collective-permute-done.1 = bf16[16,7168]{1,0:T(8,128)(2,1)S(1)} collective-permute-done((bf16[16,7168]{1,0:T(8,128)(2,1)S(1)}, bf16[16,7168]{1,0:T(8,128)(2,1)S(1)}, u32[]{:S(2)}, u32[]{:S(2)}) %collective-permute-start.1) | collective-permute-done | bytes 229408 | tf_op jit(solution)/shard_map/ppermute | solution.py:143
  19.9 0.1 add_convert_fusion
  19.9 0.1 reshape.3
  20.0 9.0 %all_to_all.11 = bf16[8,2,7168]{2,1,0:T(2,128)(2,1)S(1)} all-to-all(bf16[8,2,7168]{2,1,0:T(2,128)(2,1)S(1)} %reshape.3), channel_id=1, replica_groups={{5,4,3,0,7,6,1,2},{12,8,10,15,9,14,13,11},{21,20,19,16,23,22,17,18},{28..., dimensions={0} | all-to-all | bytes 458752 | tf_op jit(solution)/shard_map/all_to_all | solution.py:146
  29.0 0.8 %reduce_sum.12 = bf16[2,7168]{1,0:T(2,128)(2,1)} reduce(bf16[8,2,7168]{2,1,0:T(2,128)(2,1)S(1)} %all_to_all.11, bf16[]{:T(256)} %constant.2.clone.1), dimensions={0}, to_apply=%region_0.0 | reduce | flops 100352 | bytes 258050 | tf_op jit(solution)/shard_map/reduce_sum | solution.py:150
  (1 shorter events, 0.0 us)
Async XLA Ops:
  0.9 15.3 %copy-start = (bf16[1,7168,256]{2,1,0:T(8,128)(2,1)S(1)}, bf16[1,7168,256]{2,1,0:T(8,128)(2,1)}, u32[]{:S(2)}) copy-start(bf16[1,7168,256]{2,1,0:T(8,128)(2,1)} %gate_ref.1) | copy-start | bytes 11010052
  0.9 15.3 %copy-start.1 = (bf16[1,7168,256]{2,1,0:T(8,128)(2,1)S(1)}, bf16[1,7168,256]{2,1,0:T(8,128)(2,1)}, u32[]{:S(2)}) copy-start(bf16[1,7168,256]{2,1,0:T(8,128)(2,1)} %up_ref.1) | copy-start | bytes 11010052
  0.9 15.3 %copy-start.2 = (bf16[1,256,7168]{2,1,0:T(8,128)(2,1)S(1)}, bf16[1,256,7168]{2,1,0:T(8,128)(2,1)}, u32[]{:S(2)}) copy-start(bf16[1,256,7168]{2,1,0:T(8,128)(2,1)} %down_ref.1) | copy-start | bytes 11010052
  14.7 1.5 %collective-permute-start = (bf16[8,2,7296]{2,1,0:T(2,128)(2,1)S(1)}, bf16[8,2,7296]{2,1,0:T(2,128)(2,1)S(1)}, u32[]{:S(2)}, u32[]{:S(2)}) collective-permute-start(bf16[8,2,7296]{2,1,0:T(2,128)(2,1)S(1)} %all_to_all.10.own_ref), channel_id=1, source_target_pairs={{0,8},{8,0},{1,9},{9,1},{2,10},{10,2},{3,11},{11,3},{4,12},{12,4},... | collective-permute-start | bytes 700424 | tf_op jit(solution)/shard_map/ppermute | solution.py:131
  18.3 1.5 %collective-permute-start.1 = (bf16[16,7168]{1,0:T(8,128)(2,1)S(1)}, bf16[16,7168]{1,0:T(8,128)(2,1)S(1)}, u32[]{:S(2)}, u32[]{:S(2)}) collective-permute-start(bf16[16,7168]{1,0:T(8,128)(2,1)S(1)} %get-tuple-element.16), channel_id=1, source_target_pairs={{0,8},{8,0},{1,9},{9,1},{2,10},{10,2},{3,11},{11,3},{4,12},{12,4},... | collective-permute-start | bytes 688136 | tf_op jit(solution)/shard_map/ppermute | solution.py:143

commit v10 on v9

--- a/solution.py
+++ b/solution.py
@@ -11,7 +11,7 @@
 SPARE = 2048
 SPACER_LIMIT = 38 * 1024 * 1024
 COLUMNS = 1024
-SEND_ORDERS = ((5, 7, 4, 0, 3, 1, 2, 6), (5, 0, 3, 2, 4, 1, 7, 6))
+SEND_ORDERS = ((5, 7, 4, 0, 3, 1, 2, 6), (5, 6, 0, 2, 4, 3, 7, 1))
 RETURN_ORDERS = ((5, 4, 3, 0, 7, 6, 1, 2), (4, 0, 2, 7, 1, 6, 5, 3))
 
 

time: 30.1 us -> 30.1 us (level)
  no operation moved by 1% of the time
where the time goes in v10:
time: 30.1 us; the launch traced here: 29.8 us
  blocking collectives  22.8 us (76%)
  Pallas kernels  3.03 us (10%)
  waiting for transfers between devices  2.85 us (9%)
  other arithmetic  0.87 us (3%)
    all_to_all x1, blocking collectives, per_device(): lax.all_to_all(packed, ('node', 'dev'), split_axis=0, concat_axis=0, tile...  13.8 us
    all_to_all x1, blocking collectives, per_device(): lax.all_to_all(partial, ('node', 'dev'), split_axis=0, concat_axis=0, til...  8.97 us
    pallas_call x1, Pallas kernels, per_device(): pl.pallas_call(expert_kernel, out_shape=(jax.ShapeDtypeStruct((devs * tok...  2.12 us
    ppermute x1, waiting for transfers between devices, per_device(): other = lax.ppermute(own, 'node', swap)  1.49 us
    ppermute x1, waiting for transfers between devices, per_device(): arrived = lax.ppermute(other_out, 'node', swap)  1.36 us
    pallas_call x1, Pallas kernels, per_device(): pl.pallas_call(pack_kernel, out_shape=(pltpu.VMEM((devs, tok_rows, wide),...  0.91 us
    reduce_sum x1, other arithmetic, per_device(): return jnp.sum(returned.astype(jnp.float32), axis=0).astype(jnp.bfloat16)  0.82 us
  transfers between devices with their start and end apart: 2, of which 2 were waited for; matrix products, arithmetic and copies ran while one was open for 0% of the time, Pallas kernels for 0%

profile of v10, /device:TPU:0, one launch (start us, length us, event | category | flops | bytes accessed | tf_op | source)
XLA Modules:
  0.0 29.8 jit_solution(17296405106572039816)
XLA Ops:
  0.0 0.9 %pack.1 = (bf16[8,2,7296]{2,1,0:T(2,128)(2,1)S(1)}, bf16[2048,7168]{1,0:T(8,128)(2,1)}) custom-call(bf16[2,7168]{1,0:T(2,128)(2,1)} %tokens_ref.1, s32[1,2]{1,0:T(1,128)} %bitcast.1, bf16[2,1]{1,0:T(2,128)(2,1)} %weights_ref.1), custom_call_target="tpu_custom_call" | custom-call | tf_op jit(solution)/shard_map/pack/pallas_call | solution.py:108
  0.9 0.0 copy-start
  0.9 0.0 copy-start.1
  0.9 0.0 copy-start.2
  0.9 13.8 %all_to_all.10.own_ref = bf16[8,2,7296]{2,1,0:T(2,128)(2,1)S(1)} all-to-all(bf16[8,2,7296]{2,1,0:T(2,128)(2,1)S(1)} %get-tuple-element.13.packed_ref), channel_id=1, replica_groups={{5,7,4,0,3,1,2,6},{13,14,8,10,12,11,15,9},{21,23,20,16,19,17,18,22},{29..., dimensions={0} | all-to-all | bytes 466944 | tf_op jit(solution)/shard_map/all_to_all | solution.py:127
  14.7 0.0 collective-permute-start
  14.7 1.5 %collective-permute-done.other_ref = bf16[8,2,7296]{2,1,0:T(2,128)(2,1)S(1)} collective-permute-done((bf16[8,2,7296]{2,1,0:T(2,128)(2,1)S(1)}, bf16[8,2,7296]{2,1,0:T(2,128)(2,1)S(1)}, u32[]{:S(2)}, u32[]{:S(2)}) %collective-permute-start) | collective-permute-done | bytes 233504 | tf_op jit(solution)/shard_map/ppermute | solution.py:131
  16.2 0.0 copy-done
  16.2 0.0 copy-done.1
  16.2 0.0 copy-done.2
  16.2 2.1 %expert.1 = (f32[16,7168]{1,0:T(8,128)S(1)}, bf16[16,7168]{1,0:T(8,128)(2,1)S(1)}) custom-call(bf16[8,2,7296]{2,1,0:T(2,128)(2,1)S(1)} %all_to_all.10.own_ref, bf16[8,2,7296]{2,1,0:T(2,128)(2,1)S(1)} %collective-permute-done.other_ref, bf16[1,7168,256]{2,1,0:T(8,128)(2,1)S(1)} %copy-done, bf16[1,7168,256]{2,1,0:T(8,128)(2,1)S(1)} %copy-done.1, ...), custom_call_target="tpu_custom_call" | custom-call | tf_op jit(solution)/shard_map/expert/pallas_call | solution.py:132
  18.4 0.2 collective-permute-start.1
  18.5 1.4 %collective-permute-done.1 = bf16[16,7168]{1,0:T(8,128)(2,1)S(1)} collective-permute-done((bf16[16,7168]{1,0:T(8,128)(2,1)S(1)}, bf16[16,7168]{1,0:T(8,128)(2,1)S(1)}, u32[]{:S(2)}, u32[]{:S(2)}) %collective-permute-start.1) | collective-permute-done | bytes 229408 | tf_op jit(solution)/shard_map/ppermute | solution.py:143
  19.9 0.1 add_convert_fusion
  20.0 0.1 reshape.3
  20.1 9.0 %all_to_all.11 = bf16[8,2,7168]{2,1,0:T(2,128)(2,1)S(1)} all-to-all(bf16[8,2,7168]{2,1,0:T(2,128)(2,1)S(1)} %reshape.3), channel_id=1, replica_groups={{5,4,3,0,7,6,1,2},{12,8,10,15,9,14,13,11},{21,20,19,16,23,22,17,18},{28..., dimensions={0} | all-to-all | bytes 458752 | tf_op jit(solution)/shard_map/all_to_all | solution.py:146
  29.0 0.8 %reduce_sum.12 = bf16[2,7168]{1,0:T(2,128)(2,1)} reduce(bf16[8,2,7168]{2,1,0:T(2,128)(2,1)S(1)} %all_to_all.11, bf16[]{:T(256)} %constant.2.clone.1), dimensions={0}, to_apply=%region_0.0 | reduce | flops 100352 | bytes 258050 | tf_op jit(solution)/shard_map/reduce_sum | solution.py:150
  (1 shorter events, 0.0 us)
Async XLA Ops:
  0.9 15.3 %copy-start = (bf16[1,7168,256]{2,1,0:T(8,128)(2,1)S(1)}, bf16[1,7168,256]{2,1,0:T(8,128)(2,1)}, u32[]{:S(2)}) copy-start(bf16[1,7168,256]{2,1,0:T(8,128)(2,1)} %gate_ref.1) | copy-start | bytes 11010052
  0.9 15.3 %copy-start.1 = (bf16[1,7168,256]{2,1,0:T(8,128)(2,1)S(1)}, bf16[1,7168,256]{2,1,0:T(8,128)(2,1)}, u32[]{:S(2)}) copy-start(bf16[1,7168,256]{2,1,0:T(8,128)(2,1)} %up_ref.1) | copy-start | bytes 11010052
  0.9 15.3 %copy-start.2 = (bf16[1,256,7168]{2,1,0:T(8,128)(2,1)S(1)}, bf16[1,256,7168]{2,1,0:T(8,128)(2,1)}, u32[]{:S(2)}) copy-start(bf16[1,256,7168]{2,1,0:T(8,128)(2,1)} %down_ref.1) | copy-start | bytes 11010052
  14.7 1.5 %collective-permute-start = (bf16[8,2,7296]{2,1,0:T(2,128)(2,1)S(1)}, bf16[8,2,7296]{2,1,0:T(2,128)(2,1)S(1)}, u32[]{:S(2)}, u32[]{:S(2)}) collective-permute-start(bf16[8,2,7296]{2,1,0:T(2,128)(2,1)S(1)} %all_to_all.10.own_ref), channel_id=1, source_target_pairs={{0,8},{8,0},{1,9},{9,1},{2,10},{10,2},{3,11},{11,3},{4,12},{12,4},... | collective-permute-start | bytes 700424 | tf_op jit(solution)/shard_map/ppermute | solution.py:131
  18.4 1.5 %collective-permute-start.1 = (bf16[16,7168]{1,0:T(8,128)(2,1)S(1)}, bf16[16,7168]{1,0:T(8,128)(2,1)S(1)}, u32[]{:S(2)}, u32[]{:S(2)}) collective-permute-start(bf16[16,7168]{1,0:T(8,128)(2,1)S(1)} %get-tuple-element.16), channel_id=1, source_target_pairs={{0,8},{8,0},{1,9},{9,1},{2,10},{10,2},{3,11},{11,3},{4,12},{12,4},... | collective-permute-start | bytes 688136 | tf_op jit(solution)/shard_map/ppermute | solution.py:143

commit v11 on v10

--- a/solution.py
+++ b/solution.py
@@ -12,7 +12,7 @@
 SPACER_LIMIT = 38 * 1024 * 1024
 COLUMNS = 1024
 SEND_ORDERS = ((5, 7, 4, 0, 3, 1, 2, 6), (5, 6, 0, 2, 4, 3, 7, 1))
-RETURN_ORDERS = ((5, 4, 3, 0, 7, 6, 1, 2), (4, 0, 2, 7, 1, 6, 5, 3))
+RETURN_ORDERS = ((5, 4, 3, 0, 7, 6, 1, 2), (4, 0, 3, 7, 1, 6, 5, 2))
 
 
 def pack_kernel(tokens_ref, routes_ref, weights_ref, packed_ref, spare_ref):

time: 30.1 us -> 30.1 us (level)
  no operation moved by 1% of the time
where the time goes in v11:
time: 30.1 us; the launch traced here: 29.8 us
  blocking collectives  22.8 us (76%)
  Pallas kernels  3.03 us (10%)
  waiting for transfers between devices  2.85 us (9%)
  other arithmetic  0.87 us (3%)
    all_to_all x1, blocking collectives, per_device(): lax.all_to_all(packed, ('node', 'dev'), split_axis=0, concat_axis=0, tile...  13.8 us
    all_to_all x1, blocking collectives, per_device(): lax.all_to_all(partial, ('node', 'dev'), split_axis=0, concat_axis=0, til...  8.97 us
    pallas_call x1, Pallas kernels, per_device(): pl.pallas_call(expert_kernel, out_shape=(jax.ShapeDtypeStruct((devs * tok...  2.12 us
    ppermute x1, waiting for transfers between devices, per_device(): other = lax.ppermute(own, 'node', swap)  1.49 us
    ppermute x1, waiting for transfers between devices, per_device(): arrived = lax.ppermute(other_out, 'node', swap)  1.36 us
    pallas_call x1, Pallas kernels, per_device(): pl.pallas_call(pack_kernel, out_shape=(pltpu.VMEM((devs, tok_rows, wide),...  0.91 us
    reduce_sum x1, other arithmetic, per_device(): return jnp.sum(returned.astype(jnp.float32), axis=0).astype(jnp.bfloat16)  0.82 us
  transfers between devices with their start and end apart: 2, of which 2 were waited for; matrix products, arithmetic and copies ran while one was open for 0% of the time, Pallas kernels for 0%

profile of v11, /device:TPU:0, one launch (start us, length us, event | category | flops | bytes accessed | tf_op | source)
XLA Modules:
  0.0 29.8 jit_solution(4336072946970539803)
XLA Ops:
  0.0 0.9 %pack.1 = (bf16[8,2,7296]{2,1,0:T(2,128)(2,1)S(1)}, bf16[2048,7168]{1,0:T(8,128)(2,1)}) custom-call(bf16[2,7168]{1,0:T(2,128)(2,1)} %tokens_ref.1, s32[1,2]{1,0:T(1,128)} %bitcast.1, bf16[2,1]{1,0:T(2,128)(2,1)} %weights_ref.1), custom_call_target="tpu_custom_call" | custom-call | tf_op jit(solution)/shard_map/pack/pallas_call | solution.py:108
  0.9 0.0 copy-start
  0.9 0.0 copy-start.1
  0.9 0.0 copy-start.2
  0.9 13.8 %all_to_all.10.own_ref = bf16[8,2,7296]{2,1,0:T(2,128)(2,1)S(1)} all-to-all(bf16[8,2,7296]{2,1,0:T(2,128)(2,1)S(1)} %get-tuple-element.13.packed_ref), channel_id=1, replica_groups={{5,7,4,0,3,1,2,6},{13,14,8,10,12,11,15,9},{21,23,20,16,19,17,18,22},{29..., dimensions={0} | all-to-all | bytes 466944 | tf_op jit(solution)/shard_map/all_to_all | solution.py:127
  14.7 0.0 collective-permute-start
  14.7 1.5 %collective-permute-done.other_ref = bf16[8,2,7296]{2,1,0:T(2,128)(2,1)S(1)} collective-permute-done((bf16[8,2,7296]{2,1,0:T(2,128)(2,1)S(1)}, bf16[8,2,7296]{2,1,0:T(2,128)(2,1)S(1)}, u32[]{:S(2)}, u32[]{:S(2)}) %collective-permute-start) | collective-permute-done | bytes 233504 | tf_op jit(solution)/shard_map/ppermute | solution.py:131
  16.2 0.0 copy-done
  16.2 0.0 copy-done.1
  16.2 0.0 copy-done.2
  16.2 2.1 %expert.1 = (f32[16,7168]{1,0:T(8,128)S(1)}, bf16[16,7168]{1,0:T(8,128)(2,1)S(1)}) custom-call(bf16[8,2,7296]{2,1,0:T(2,128)(2,1)S(1)} %all_to_all.10.own_ref, bf16[8,2,7296]{2,1,0:T(2,128)(2,1)S(1)} %collective-permute-done.other_ref, bf16[1,7168,256]{2,1,0:T(8,128)(2,1)S(1)} %copy-done, bf16[1,7168,256]{2,1,0:T(8,128)(2,1)S(1)} %copy-done.1, ...), custom_call_target="tpu_custom_call" | custom-call | tf_op jit(solution)/shard_map/expert/pallas_call | solution.py:132
  18.4 0.2 collective-permute-start.1
  18.5 1.4 %collective-permute-done.1 = bf16[16,7168]{1,0:T(8,128)(2,1)S(1)} collective-permute-done((bf16[16,7168]{1,0:T(8,128)(2,1)S(1)}, bf16[16,7168]{1,0:T(8,128)(2,1)S(1)}, u32[]{:S(2)}, u32[]{:S(2)}) %collective-permute-start.1) | collective-permute-done | bytes 229408 | tf_op jit(solution)/shard_map/ppermute | solution.py:143
  19.9 0.1 add_convert_fusion
  20.0 0.1 reshape.3
  20.1 9.0 %all_to_all.11 = bf16[8,2,7168]{2,1,0:T(2,128)(2,1)S(1)} all-to-all(bf16[8,2,7168]{2,1,0:T(2,128)(2,1)S(1)} %reshape.3), channel_id=1, replica_groups={{5,4,3,0,7,6,1,2},{12,8,11,15,9,14,13,10},{21,20,19,16,23,22,17,18},{28..., dimensions={0} | all-to-all | bytes 458752 | tf_op jit(solution)/shard_map/all_to_all | solution.py:146
  29.0 0.8 %reduce_sum.12 = bf16[2,7168]{1,0:T(2,128)(2,1)} reduce(bf16[8,2,7168]{2,1,0:T(2,128)(2,1)S(1)} %all_to_all.11, bf16[]{:T(256)} %constant.2.clone.1), dimensions={0}, to_apply=%region_0.0 | reduce | flops 100352 | bytes 258050 | tf_op jit(solution)/shard_map/reduce_sum | solution.py:150
  (1 shorter events, 0.0 us)
Async XLA Ops:
  0.9 15.3 %copy-start = (bf16[1,7168,256]{2,1,0:T(8,128)(2,1)S(1)}, bf16[1,7168,256]{2,1,0:T(8,128)(2,1)}, u32[]{:S(2)}) copy-start(bf16[1,7168,256]{2,1,0:T(8,128)(2,1)} %gate_ref.1) | copy-start | bytes 11010052
  0.9 15.3 %copy-start.1 = (bf16[1,7168,256]{2,1,0:T(8,128)(2,1)S(1)}, bf16[1,7168,256]{2,1,0:T(8,128)(2,1)}, u32[]{:S(2)}) copy-start(bf16[1,7168,256]{2,1,0:T(8,128)(2,1)} %up_ref.1) | copy-start | bytes 11010052
  0.9 15.3 %copy-start.2 = (bf16[1,256,7168]{2,1,0:T(8,128)(2,1)S(1)}, bf16[1,256,7168]{2,1,0:T(8,128)(2,1)}, u32[]{:S(2)}) copy-start(bf16[1,256,7168]{2,1,0:T(8,128)(2,1)} %down_ref.1) | copy-start | bytes 11010052
  14.7 1.5 %collective-permute-start = (bf16[8,2,7296]{2,1,0:T(2,128)(2,1)S(1)}, bf16[8,2,7296]{2,1,0:T(2,128)(2,1)S(1)}, u32[]{:S(2)}, u32[]{:S(2)}) collective-permute-start(bf16[8,2,7296]{2,1,0:T(2,128)(2,1)S(1)} %all_to_all.10.own_ref), channel_id=1, source_target_pairs={{0,8},{8,0},{1,9},{9,1},{2,10},{10,2},{3,11},{11,3},{4,12},{12,4},... | collective-permute-start | bytes 700424 | tf_op jit(solution)/shard_map/ppermute | solution.py:131
  18.4 1.5 %collective-permute-start.1 = (bf16[16,7168]{1,0:T(8,128)(2,1)S(1)}, bf16[16,7168]{1,0:T(8,128)(2,1)S(1)}, u32[]{:S(2)}, u32[]{:S(2)}) collective-permute-start(bf16[16,7168]{1,0:T(8,128)(2,1)S(1)} %get-tuple-element.16), channel_id=1, source_target_pairs={{0,8},{8,0},{1,9},{9,1},{2,10},{10,2},{3,11},{11,3},{4,12},{12,4},... | collective-permute-start | bytes 688136 | tf_op jit(solution)/shard_map/ppermute | solution.py:143
